TPU v7x, 32 devices: a whole 2x2x4 slice. The times are simulated.
32 devices in a mesh: row: 8 (over y, x, core), col: 4 (over z).
Axes of the slice: x: 2, y: 2, z: 4, core: 2. Of those that a mesh axis runs over, the one named last changes fastest.
Arguments:
- object_field: float32 [2, 3072, 1536], P(None, 'row', 'col'), may hold values from -6 to 6
- probe: float32 [2, 128, 128], replicated, may hold values from -6 to 6
- amplitudes: float32 [8, 4, 12, 128, 128], P('row', 'col'), may hold values from 0.2 to 4
- offsets: int32 [8, 4, 12, 2], P('row', 'col'), may hold values from -64 to 319
- counts: int32 [8, 4], P('row', 'col'), may hold values from 1 to 12, as said below
Outputs:
- updated_object: float32 [2, 3072, 1536], P(None, 'row', 'col')
Inputs may be any that keep to these rules, and one draw needn't show every extreme that they name: `counts`: some tile has exactly 12 live positions in every draw.
All inputs are finite; a program needn't handle non-finite values.
Results may differ from a plain program's by a relative error of at most 0.0001.
Values sent between devices are 32-bit elements; how exact they have to be, the bound alone decides.
No kernel may reach another device: no remote copies, remote signals or barrier semaphores. Data moves between devices by JAX's collectives and lax.ppermute only.
A program may use at most 64 MiB of HBM per device.

v0:
```python
import functools
import math

import jax
import jax.numpy as jnp
import numpy as np
from jax import lax
from jax.experimental import pallas as pl
from jax.experimental.pallas import tpu as pltpu
from jax.sharding import PartitionSpec as P

ITERS = 2
FLOOR = 0.25
VMEM_BYTES = 16 * 1024 * 1024
GROUP = 4
CHAIN = 2


def split(value):
    high = value.astype(jnp.bfloat16)
    low = (value - high.astype(jnp.float32)).astype(jnp.bfloat16)
    return high, low


def dft_tables(length):
    index = np.arange(length)
    angle = (index[:, None] * index[None, :] % length) * (2.0 * math.pi / length)
    cosine = np.cos(angle) / math.sqrt(length)
    sine = np.sin(angle) / math.sqrt(length)
    ahead = np.block([[cosine, -sine], [sine, cosine]])
    parts = []
    for table in (ahead, ahead.T):
        high = table.astype(jnp.bfloat16)
        low = (table - high.astype(np.float64)).astype(jnp.bfloat16)
        parts += [high, low]
    return np.stack(parts)


def lanes(shape):
    return lax.broadcasted_iota(jnp.int32, shape, len(shape) - 1)


def swap(value, half):
    return pltpu.roll(value, half, value.ndim - 1)


def odd_place(axis):
    return lax.axis_index(axis) % 2 == 1


def by_pairs(axis, low, high):
    odd = odd_place(axis)
    return jnp.where(odd, high, low), jnp.where(odd, low, high)


def by_side(axis, first, second):
    odd = odd_place(axis)
    return jnp.where(odd, second, first), jnp.where(odd, first, second)


def times_right(rows, high, low):
    top, rest = split(rows)
    left = jnp.concatenate([top, top, rest], axis=1)
    right = jnp.concatenate([high, low, high], axis=0)
    return jnp.dot(left, right, preferred_element_type=jnp.float32)


def times_left(high, low, columns):
    top, rest = split(columns)
    left = jnp.concatenate([high, low, high], axis=1)
    right = jnp.concatenate([top, top, rest], axis=0)
    return jnp.dot(left, right, preferred_element_type=jnp.float32)


def beside(left, right):
    return jnp.concatenate([left, right], axis=1)


def above(top, bottom):
    return jnp.concatenate([top, bottom], axis=0)


def touching(mid_row, mid_col, cross_row, cross_col):
    return ~(mid_row & mid_col) & (cross_row | cross_col)


def early(mid_row, mid_col, cross_row, cross_col):
    return ~(mid_row & mid_col) & ~(cross_row | cross_col)


def clear(mid_row, mid_col, cross_row, cross_col):
    return mid_row & mid_col


def collect(chosen, found, offsets, counts, tile, length, wanted, begin=0, end=None):
    last = tile - length
    half = length // 2

    def look(slot, carry):
        found, seen = carry
        row = offsets[0, 0, 0, slot]
        col = offsets[0, 0, 1, slot]
        taken = wanted(
            mid_row=(row >= half) & (row <= last - half),
            mid_col=(col >= half) & (col <= last - half),
            cross_row=(row < 0) | (row > last),
            cross_col=(col < 0) | (col > last),
        )
        listed = taken & (seen >= begin)
        if end is not None:
            listed = listed & (seen < end)
        chosen[found] = slot
        return found + jnp.where(listed, 1, 0), seen + jnp.where(taken, 1, 0)

    return lax.fori_loop(0, counts[0, 0], look, (found, 0))


def early_list(chosen, *place):
    found, known = collect(chosen, 0, *place, early, 0, GROUP)
    found, _ = collect(chosen, found, *place, clear, 0, GROUP - jnp.minimum(known, GROUP))
    return found


def first_list(chosen, *place):
    found, _ = collect(chosen, 0, *place, touching)
    found, known = collect(chosen, found, *place, early, GROUP)
    begin = GROUP - jnp.minimum(known, GROUP)
    end = begin + lax.rem(GROUP - lax.rem(found, GROUP), GROUP)
    found, _ = collect(chosen, found, *place, clear, begin, end)
    return found, end


def choose(chosen, *place):
    found, _ = collect(chosen, 0, *place)
    return found


def add_gradients(frame, acc, probe_ref, amps, offsets, tables, chosen, found, own_frame=False, own_acc=False):
    length = probe_ref.shape[-1]
    half = length // 2
    lane = lanes((length, length))

    def place(slot, ref, own):
        col = offsets[0, 0, 1, slot] + length
        block = lax.div(col, length)
        row = offsets[0, 0, 0, slot]
        if own:
            block = block - 1
        else:
            row = row + half
        after = jnp.minimum(block + 1, ref.shape[1] - 1)
        return pl.ds(row, length), block, after, lax.rem(col, length)

    def exit_wave(slot):
        at, block, after, shift = place(slot, frame, own_frame)
        inside = lane >= shift
        window = [
            jnp.where(inside, frame[part, block, at, :], frame[part, after, at, :])
            for part in (0, 1)
        ]
        probe = (pltpu.roll(probe_ref[0], shift, 1), pltpu.roll(probe_ref[1], shift, 1))
        wave = (probe[0] * window[0] - probe[1] * window[1],
                probe[0] * window[1] + probe[1] * window[0])
        return probe, wave

    def shrink(real, imag, slot):
        ratio = amps[0, 0, slot] * lax.rsqrt(real * real + imag * imag + FLOOR) - 1.0
        return real * ratio, imag * ratio

    def put(slot, live, probe, back_r, back_i):
        at, block, after, shift = place(slot, acc, own_acc)
        grads = (probe[0] * back_r + probe[1] * back_i, probe[0] * back_i - probe[1] * back_r)
        bound = jnp.where(live, shift, length)
        inside = lane >= bound
        beyond = lane < jnp.where(live, shift, 0)
        for part in (0, 1):
            acc[part, block, at, :] += jnp.where(inside, grads[part], 0.0)
            acc[part, after, at, :] += jnp.where(beyond, grads[part], 0.0)

    def work(slots):
        probes, waves = zip(*[exit_wave(slot) for slot in slots])
        rows = jnp.concatenate([beside(*wave) for wave in waves], axis=0)
        mid = times_right(rows, tables[0], tables[1])
        yield None
        mids = [mid[k * length:(k + 1) * length] for k in range(len(slots))]
        columns = above(
            jnp.concatenate([m[:, :length] for m in mids], axis=1),
            jnp.concatenate([m[:, length:] for m in mids], axis=1),
        )
        far = times_left(tables[2], tables[3], columns)
        yield None
        changes = [
            shrink(far[:length, k * length:(k + 1) * length],
                   far[length:, k * length:(k + 1) * length], slot)
            for k, slot in enumerate(slots)
        ]
        columns = above(
            jnp.concatenate([c[0] for c in changes], axis=1),
            jnp.concatenate([c[1] for c in changes], axis=1),
        )
        mid = times_left(tables[0], tables[1], columns)
        yield None
        rows = jnp.concatenate(
            [
                beside(mid[:length, k * length:(k + 1) * length],
                       mid[length:, k * length:(k + 1) * length])
                for k in range(len(slots))
            ],
            axis=0,
        )
        back = times_right(rows, tables[2], tables[3])
        yield None
        yield [
            (probes[k], back[k * length:(k + 1) * length, :length],
             back[k * length:(k + 1) * length, length:])
            for k in range(len(slots))
        ]

    def step(index, carry):
        places = [index * GROUP + k for k in range(GROUP)]
        slots = [chosen[jnp.where(at < found, at, 0)] for at in places]
        chains = [work(slots[k:k + CHAIN]) for k in range(0, GROUP, CHAIN)]
        gradients = [None]
        while gradients[0] is None:
            gradients = [next(chain) for chain in chains]
        gradients = [gradient for chain in gradients for gradient in chain]
        for at, slot, gradient in zip(places, slots, gradients):
            put(slot, at < found, *gradient)
        return carry

    lax.fori_loop(0, (found + GROUP - 1) // GROUP, step, 0)


def start_pass(field, offsets_from, counts, tile_out, cols_a, cols_b, rows_a, rows_b, offsets, sems):
    _, nb, tile, length = tile_out.shape
    half = length // 2
    npos = offsets.shape[3]
    listed = pltpu.make_async_copy(offsets_from, offsets, sems.at[nb])
    listed.start()
    copies = [
        pltpu.make_async_copy(
            field.at[:, :, b * length:(b + 1) * length], tile_out.at[:, b], sems.at[b])
        for b in range(nb)
    ]
    for copy in copies:
        copy.start()
    listed.wait()
    spot = lanes((8, length))
    info = jnp.zeros((8, length), jnp.int32)
    down = (lax.axis_index("row") + 1) * tile
    across = (lax.axis_index("col") + 1) * tile
    for k in range(npos):
        live = k < counts[0, 0]
        info = jnp.where(spot == k, jnp.where(live, offsets[0, 0, 0, k] + down, 0), info)
        info = jnp.where(spot == npos + k, jnp.where(live, offsets[0, 0, 1, k] + across, 0), info)
    info = info.astype(jnp.float32)
    for end in (cols_a, cols_b, rows_a, rows_b):
        end[pl.ds(end.shape[0] - 8, 8), :] = info
    for copy in copies:
        copy.wait()
    low = lanes((tile, length)) < half
    to_left = jnp.where(low, tile_out[0, 0], swap(tile_out[1, 0], half))
    to_right = jnp.where(low, swap(tile_out[1, nb - 1], half), tile_out[0, nb - 1])
    cols_a[:tile], cols_b[:tile] = by_pairs("col", to_left, to_right)
    for part in (0, 1):
        for b in range(nb):
            at = pl.ds((part * nb + b) * half, half)
            rows_a[at, :], rows_b[at, :] = by_pairs(
                "row", tile_out[part, b, :half], tile_out[part, b, tile - half:])


def start_corners(cols_a, cols_b, after, corners_a, corners_b):
    length = cols_a.shape[1]
    half = length // 2
    tile = cols_a.shape[0] - 8
    low = lanes((tile, length)) < half
    left, right = by_side("col", cols_a[:tile], cols_b[:tile])
    for part in (0, 1):
        if part:
            left, right = swap(left, half), swap(right, half)
        value = jnp.where(low, right, left)
        at = pl.ds(part * half, half)
        corners_a[at, :], corners_b[at, :] = by_pairs("row", value[:half], value[tile - half:])
    first = lax.broadcasted_iota(jnp.int32, (8, length), 0) == 0
    info = jnp.where(first, cols_a[tile:], cols_b[tile:])
    corners_a[2 * half:] = info
    corners_b[2 * half:] = info


def fetch_pass(after, probe_from, amps_from, tables_from, probe, amps, tables, sems):
    copies = [
        pltpu.make_async_copy(source, target, sems.at[k])
        for k, (source, target) in enumerate(
            ((amps_from, amps), (tables_from, tables), (probe_from, probe)))
    ]
    for copy in copies:
        copy.start()
    for copy in copies:
        copy.wait()


def early_pass(offsets, counts, after, field, probe, amps, tables, acc, chosen):
    _, nb, tile, length = field.shape
    acc[...] = jnp.zeros_like(acc)
    found = early_list(chosen, offsets, counts, tile, length)
    add_gradients(field, acc, probe, amps, offsets, tables, chosen, found,
                  own_frame=True, own_acc=True)


def first_pass(offsets, counts, field, done, cols_a, cols_b, rows_a, rows_b, corners_a, corners_b,
               probe, amps, tables, frame, acc, tips_a, tips_b, sums_a, sums_b, edges_a, edges_b, chosen):
    _, nb, tile, length = field.shape
    half = length // 2
    rows = tile + 2 * half
    own = pl.ds(half, tile)
    left, right = by_side("col", cols_a[:tile], cols_b[:tile])
    top = pl.ds(0, half)
    bottom = pl.ds(half + tile, half)
    for part in (0, 1):
        for b in range(nb):
            frame[part, b + 1, own, :] = field[part, b]
            at = pl.ds((part * nb + b) * half, half)
            frame[part, b + 1, top, :], frame[part, b + 1, bottom, :] = by_side(
                "row", rows_a[at, :], rows_b[at, :])
        frame[part, 0, own, :] = swap(left, half) if part else left
        frame[part, nb + 1, own, :] = swap(right, half) if part else right
        at = pl.ds(part * half, half)
        ends = by_side("row", corners_a[at, :], corners_b[at, :])
        for block in (0, nb + 1):
            frame[part, block, top, :], frame[part, block, bottom, :] = ends
    empty = jnp.zeros((half, length), jnp.float32)
    for part in (0, 1):
        for b in range(nb + 2):
            acc[part, b, top, :] = empty
            acc[part, b, bottom, :] = empty
            acc[part, b, own, :] = (
                done[part, b - 1] if 0 < b <= nb else jnp.zeros((tile, length), jnp.float32))
    found, _ = first_list(chosen, offsets, counts, tile, length)
    add_gradients(frame, acc, probe, amps, offsets, tables, chosen, found)
    low = lanes((rows, length)) < half
    for part in (0, 1):
        strip_a, strip_b = by_pairs(
            "col",
            jnp.where(low, acc[part, 1], acc[part, 0]),
            jnp.where(low, acc[part, nb + 1], acc[part, nb]),
        )
        for strip, tips, sums in ((strip_a, tips_a, sums_a), (strip_b, tips_b, sums_b)):
            tips[part, 0] = strip[:length]
            tips[part, 1] = strip[rows - length:]
            sums[part] = strip[length:rows - length]
    near = lanes((length, length)) < half
    for part in (0, 1):
        for b in range(nb - 1):
            ends = [
                acc[part, b + 2, at, :] if b < nb - 2
                else jnp.where(near, acc[part, nb, at, :], acc[part, 1, at, :])
                for at in (pl.ds(0, length), pl.ds(rows - length, length))
            ]
            edges_a[part, b], edges_b[part, b] = by_pairs("row", *ends)


def middle_corners(mine_a, mine_b, tips_a, tips_b, after, corners, *, odd_pairs):
    for part in (0, 1):
        up, down = [
            by_side("col", mine_a[part, k] + tips_a[part, k], mine_b[part, k] + tips_b[part, k])
            for k in (0, 1)
        ]
        for side in (0, 1):
            corners[part, side] = by_pairs("row", up[side], down[side])[0 if odd_pairs else 1]


def light_pass(mine, cols_a, cols_b, rows_a, rows_b, corners_a, corners_b, probe, after,
               inverse, light, power, places, listed, chosen, sem, *, npos):
    length = probe.shape[-1]
    half = length // 2
    blocks, rows, _ = inverse.shape
    nb = blocks - 2
    tile = nb * length
    my_row = lax.axis_index("row")
    my_col = lax.axis_index("col")
    sources = (mine, cols_a, cols_b, rows_a, rows_b, corners_a, corners_b)
    for k, source in enumerate(sources):
        given = source[source.shape[0] - 8:, :].astype(jnp.int32)
        col = pltpu.roll(given, length - npos, 1) - (my_col + 1) * tile + 2 * length
        row = given - (my_row + 1) * tile + half + length
        near = (given > 0) & (row > 0) & (row < rows + length)
        near = near & (col > length - half) & (col < 2 * length + tile + half)
        places[pl.ds(8 * k, 8), :] = jnp.where(near, row * 4 * tile + col, 0)
    copy = pltpu.make_async_copy(places, listed, sem)
    copy.start()
    for b in range(blocks):
        light[b + 1, pl.ds(length, rows), :] = jnp.zeros((rows, length), jnp.float32)
    power[...] = probe[0] * probe[0] + probe[1] * probe[1]
    lane = lanes((length, length))
    copy.wait()

    def look(index, found):
        line = jnp.where(index < len(sources), 8 * index, 8 * (index - 2) + 1)
        for slot in range(npos):
            place = listed[line, slot]
            chosen[found] = place
            found = found + jnp.where(place > 0, 1, 0)
        return found

    found = lax.fori_loop(0, len(sources) + 2, look, 0)

    def put(index, carry):
        place = chosen[index]
        start = lax.div(place, 4 * tile)
        col = lax.rem(place, 4 * tile)
        block = lax.div(col, length)
        shift = lax.rem(col, length)
        value = pltpu.roll(power[...], shift, 1)
        inside = lane >= shift
        light[block, pl.ds(start, length), :] += jnp.where(inside, value, 0.0)
        light[block + 1, pl.ds(start, length), :] += jnp.where(inside, 0.0, value)
        return carry

    lax.fori_loop(0, found, put, 0)
    spot = lax.broadcasted_iota(jnp.int32, (rows, length), 0)
    keep_from = jnp.where(my_row > 0, 0, half)
    keep_to = jnp.where(my_row < lax.axis_size("row") - 1, rows, rows - half)
    kept = (spot >= keep_from) & (spot < keep_to)
    for b in range(blocks):
        value = 1.0 / (light[b + 1, pl.ds(length, rows), :] + 1.0)
        keep = kept
        if b == 0:
            keep = keep & (my_col > 0)
        if b == nb + 1:
            keep = keep & (my_col < lax.axis_size("col") - 1)
        inverse[b] = jnp.where(keep, value, 0.0)


def update_pass(offsets, counts, after, frame, acc, inverse, tips_a, tips_b, sums_a, sums_b, probe, amps, tables,
                work, total, chosen):
    _, blocks, rows, length = frame.shape
    half = length // 2
    nb = blocks - 2
    work[...] = acc[...]
    _, done = first_list(chosen, offsets, counts, nb * length, length)
    found, _ = collect(chosen, 0, offsets, counts, nb * length, length, clear, done)
    add_gradients(frame, work, probe, amps, offsets, tables, chosen, found)
    low = lanes((rows, length)) < half
    for part in (0, 1):
        left, right = by_side("col", *[
            above(above(tips[part, 0], sums[part]), tips[part, 1])
            for tips, sums in ((tips_a, sums_a), (tips_b, sums_b))
        ])
        for b in range(blocks):
            value = work[part, b]
            if b == 0:
                value = value + left
            if b == 1:
                value = value + jnp.where(low, left, 0.0)
            if b == nb:
                value = value + jnp.where(low, 0.0, right)
            if b == nb + 1:
                value = value + right
            work[part, b] = frame[part, b] + value * inverse[b]
    total[...] = jnp.zeros_like(total)
    found = choose(chosen, offsets, counts, nb * length, length, lambda mid_row, **_: mid_row)
    add_gradients(work, total, probe, amps, offsets, tables, chosen, found)


def second_pass(offsets, counts, work_from, total_from, inverse, edges_a, edges_b,
                corners_a, corners_b, probe, amps, tables,
                work, sums, cols_a, cols_b, rows_a, rows_b, total, chosen):
    _, blocks, rows, length = work.shape
    half = length // 2
    nb = blocks - 2
    tile = nb * length
    near = lanes((length, length)) < half
    middle = pl.ds(length, rows - 2 * length)
    for part in (0, 1):
        edges = [by_side("row", edges_a[part, b], edges_b[part, b]) for b in range(nb - 1)]
        corners = [by_side("row", corners_a[part, side], corners_b[part, side]) for side in (0, 1)]
        for k, at in enumerate((pl.ds(0, length), pl.ds(rows - length, length))):
            left, right, ends = corners[0][k], corners[1][k], edges[nb - 2][k]
            add = [left, jnp.where(near, left, ends)]
            add += [edges[b][k] for b in range(nb - 2)]
            add += [jnp.where(near, ends, right), right]
            for b in range(blocks):
                work[part, b, at, :] = work_from[part, b, at, :] + add[b] * inverse[b, at, :]
        for b in range(blocks):
            work[part, b, middle, :] = work_from[part, b, middle, :]
    total[...] = total_from[...]
    found = choose(
        chosen, offsets, counts, tile, length,
        lambda mid_row, cross_row, cross_col, **_: ~mid_row & (cross_row | cross_col))
    add_gradients(work, total, probe, amps, offsets, tables, chosen, found)
    low = lanes((rows, length)) < half
    cols_a[...], cols_b[...] = by_pairs(
        "col",
        jnp.where(low, swap(total[1, 0], half), total[0, 0]),
        jnp.where(low, total[0, nb + 1], swap(total[1, nb + 1], half)),
    )
    for part in (0, 1):
        for b in range(nb):
            sums[part, b] = total[part, b + 1, pl.ds(half, tile), :]
            rows_a[part, b], rows_b[part, b] = by_pairs(
                "row", total[part, b + 1, :half, :], total[part, b + 1, half + tile:, :])


def inner_pass(offsets, counts, work, probe, amps, tables, sums, chosen):
    _, nb, tile, length = sums.shape
    sums[...] = jnp.zeros_like(sums)
    found = choose(
        chosen, offsets, counts, tile, length,
        lambda mid_row, cross_row, cross_col, **_: ~mid_row & ~cross_row & ~cross_col)
    add_gradients(work, sums, probe, amps, offsets, tables, chosen, found, own_acc=True)


def end_corners(cols_a, cols_b, corners_a, corners_b):
    rows, length = cols_a.shape
    half = length // 2
    for side, value in enumerate(by_side("col", cols_a[...], cols_b[...])):
        corners_a[side], corners_b[side] = by_pairs("row", value[:half], value[rows - half:])


def last_pass(work, sums, inner, inverse, cols_a, cols_b, rows_a, rows_b, corners_a, corners_b,
              out, result, sems):
    _, nb, tile, length = sums.shape
    half = length // 2
    low = lanes((tile, length)) < half
    own = pl.ds(half, tile)
    gap = jnp.zeros((tile - 2 * half, length), jnp.float32)
    sides = []
    for side, value in enumerate(by_side("col", cols_a[own, :], cols_b[own, :])):
        up, down = by_side("row", corners_a[side], corners_b[side])
        sides.append(value + above(above(up, gap), down))
    left, right = sides
    copies = []
    for part in (0, 1):
        if part:
            left, right = swap(left, half), swap(right, half)
        for b in range(nb):
            up, down = by_side("row", rows_a[part, b], rows_b[part, b])
            value = sums[part, b] + inner[part, b] + above(above(up, gap), down)
            if b == 0:
                value = value + jnp.where(low, left, 0.0)
            if b == nb - 1:
                value = value + jnp.where(low, 0.0, right)
            result[part, b] = work[part, b + 1, own, :] + value * inverse[b + 1, own, :]
            copy = pltpu.make_async_copy(
                result.at[part, b], out.at[part, :, b * length:(b + 1) * length],
                sems.at[part * nb + b])
            copy.start()
            copies.append(copy)
    for copy in copies:
        copy.wait()


def whole(memory_space=pltpu.VMEM):
    return pl.BlockSpec(memory_space=memory_space)


def call(body, shapes, places, scratch=(), cost=None):
    return pl.pallas_call(
        body,
        out_shape=[jax.ShapeDtypeStruct(shape, jnp.float32) for shape in shapes],
        in_specs=[whole({"s": pltpu.SMEM, "v": pltpu.VMEM, "a": pl.ANY, "h": pltpu.HBM}[p]) for p in places],
        out_specs=[whole()] * len(shapes),
        scratch_shapes=list(scratch),
        compiler_params=pltpu.CompilerParams(vmem_limit_bytes=VMEM_BYTES),
        cost_estimate=cost,
    )


def swap_pairs(first, second, axis):
    count = lax.axis_size(axis)
    got = []
    for value, start in ((first, 1), (second, 0)):
        pairs = [(i, i + 1) for i in range(start, count - 1, 2)]
        got.append(lax.ppermute(value, axis, pairs + [(b, a) for a, b in pairs]))
    return got


def shards(object_field, probe, amplitudes, offsets, counts):
    length = probe.shape[-1]
    half = length // 2
    tile = object_field.shape[1]
    npos = offsets.shape[2]
    nb = tile // length
    blocks = nb + 2
    rows = tile + 2 * half
    tables = jnp.asarray(dft_tables(length))
    offsets = jnp.swapaxes(offsets, 2, 3)

    def cost(positions):
        steps = 4 * 3 * 2 * length * (2 * length) ** 2
        return pl.CostEstimate(
            flops=positions * steps, bytes_accessed=8_000_000,
            transcendentals=positions * length * length)

    memory = pltpu.VMEM
    chosen = pltpu.SMEM((npos + GROUP,), jnp.int32)
    strip = (tile + 8, length)
    edge = (2 * nb * half + 8, length)
    def kept(array):
        return pltpu.with_memory_space_constraint(array, pltpu.HBM)

    field, cols_a, cols_b, rows_a, rows_b = call(
        start_pass, [(2, nb, tile, length), strip, strip, edge, edge], "hhs",
        [pltpu.SMEM((1, 1, 2, npos), jnp.int32), pltpu.SemaphoreType.DMA((nb + 1,))],
    )(kept(object_field), kept(offsets), counts)
    mine = cols_a
    probe, amplitudes, tables = pl.pallas_call(
        fetch_pass,
        out_shape=[
            jax.ShapeDtypeStruct(array.shape, array.dtype) for array in (probe, amplitudes, tables)],
        in_specs=[whole(pl.ANY)] + [whole(pltpu.HBM)] * 3,
        out_specs=[whole()] * 3,
        scratch_shapes=[pltpu.SemaphoreType.DMA((3,))],
        compiler_params=pltpu.CompilerParams(vmem_limit_bytes=VMEM_BYTES),
        cost_estimate=cost(1),
    )(cols_a, kept(probe), kept(amplitudes), kept(tables))
    cols_a, cols_b = swap_pairs(cols_a, cols_b, "col")
    rows_a, rows_b = swap_pairs(rows_a, rows_b, "row")
    corner = (2 * half + 8, length)
    corners_a, corners_b = call(start_corners, [corner, corner], "vva")(cols_a, cols_b, probe)
    (done,) = call(
        early_pass, [(2, nb, tile, length)], "ssavvvv", [chosen], cost(GROUP),
    )(offsets, counts, corners_b, field, probe, amplitudes, tables)
    corners_a, corners_b = swap_pairs(corners_a, corners_b, "row")

    full = (2, blocks, rows, length)
    strip = (2, rows, length)
    edge = (2, nb - 1, length, length)
    tip = (2, 2, length, length)
    strip = (2, rows - 2 * length, length)
    frame, acc, tips_a, tips_b, sums_a, sums_b, edges_a, edges_b = call(
        first_pass, [full, full, tip, tip, strip, strip, edge, edge], "ss" + 11 * "v", [chosen],
    )(offsets, counts, field, done, cols_a, cols_b, rows_a, rows_b, corners_a, corners_b,
      probe, amplitudes, tables)
    info = (mine, cols_a, cols_b, rows_a, rows_b, corners_a, corners_b)
    mine_a, mine_b = tips_a, tips_b
    tips_a, tips_b = swap_pairs(tips_a, tips_b, "col")
    edges_a, edges_b = swap_pairs(edges_a, edges_b, "row")
    sums_a, sums_b = swap_pairs(sums_a, sums_b, "col")
    (inverse,) = call(
        functools.partial(light_pass, npos=npos), [(blocks, rows, length)], 8 * "v" + "a",
        [memory((blocks + 2, rows + 2 * length, length), jnp.float32),
         memory((length, length), jnp.float32), memory((7 * 8, length), jnp.int32),
         pltpu.SMEM((7 * 8, length), jnp.int32), pltpu.SMEM((9 * npos + 1,), jnp.int32),
         pltpu.SemaphoreType.DMA],
        cost(npos // 2),
    )(*info, probe, tips_b)
    corners_a, corners_b = [
        call(functools.partial(middle_corners, odd_pairs=odd_pairs), [tip], "vvvva")(
            mine_a, mine_b, tips_a, tips_b, after)[0]
        for odd_pairs, after in ((True, acc), (False, inverse))
    ]
    corners_a, corners_b = swap_pairs(corners_a, corners_b, "row")

    work, total = call(update_pass, [full, full], "ssa" + 10 * "v", [chosen], cost(npos // 2))(
        offsets, counts, edges_a, frame, acc, inverse, tips_a, tips_b, sums_a, sums_b,
        probe, amplitudes, tables)
    strip = (rows, length)
    own = (2, nb, tile, length)
    edge = (2, nb, half, length)
    work, sums, cols_a, cols_b, rows_a, rows_b = call(
        second_pass, [full, own, strip, strip, edge, edge], "ss" + 10 * "v",
        [memory(full, jnp.float32), chosen], cost(npos // 2),
    )(offsets, counts, work, total, inverse, edges_a, edges_b, corners_a, corners_b,
      probe, amplitudes, tables)
    cols_a, cols_b = swap_pairs(cols_a, cols_b, "col")
    rows_a, rows_b = swap_pairs(rows_a, rows_b, "row")
    (inner,) = call(inner_pass, [own], "ss" + 4 * "v", [chosen], cost(npos // 4))(
        offsets, counts, work, probe, amplitudes, tables)
    corner = (2, half, length)
    corners_a, corners_b = call(end_corners, [corner, corner], "vv")(cols_a, cols_b)
    corners_a, corners_b = swap_pairs(corners_a, corners_b, "row")
    out = pl.pallas_call(
        last_pass,
        out_shape=jax.ShapeDtypeStruct((2, tile, tile), jnp.float32),
        in_specs=[whole()] * 10,
        out_specs=whole(pl.ANY),
        scratch_shapes=[memory(own, jnp.float32), pltpu.SemaphoreType.DMA((2 * nb,))],
        compiler_params=pltpu.CompilerParams(vmem_limit_bytes=VMEM_BYTES),
    )(work, sums, inner, inverse, cols_a, cols_b, rows_a, rows_b, corners_a, corners_b)
    return out


def solution(mesh):
    placed = (
        P(None, "row", "col"),
        P(),
        P("row", "col", None, None, None),
        P("row", "col", None, None),
        P("row", "col"),
    )
    return jax.shard_map(
        shards, mesh=mesh, in_specs=placed, out_specs=P(None, "row", "col"), check_vma=False
    )
```

profile of v0, /device:TPU:4, one launch (start us, length us, event | category | flops | bytes accessed | tf_op | source)
XLA Modules:
  0.0 67.2 jit_solution(10534634584728426116)
XLA Ops:
  0.7 1.5 %shard_map.64 = (f32[2,3,384,128]{3,2,1,0:T(8,128)S(1)}, f32[392,128]{1,0:T(8,128)S(1)}, f32[392,128]{1,0:T(8,128)S(1)}, f32[392,128]{1,0:T(8,128)S(1)}, f32[392,128]{1,0:T(8,128)S(1)}) custom-call(f32[2,384,384]{2,1,0:T(8,128)} %field.1, s32[1,1,2,12]{3,2,1,0:T(2,128)} %bitcast.1, s32[1,1]{1,0:T(1,128)S(6)} %copy.7.counts), custom_call_target="tpu_custom_call" | custom-call | tf_op jit(solution)/shard_map/pallas_call | solution.py:602
  2.2 1.6 %collective-permute-start.1 = (f32[392,128]{1,0:T(8,128)S(1)}, f32[392,128]{1,0:T(8,128)S(1)}, u32[]{:S(2)}, u32[]{:S(2)}) collective-permute-start(f32[392,128]{1,0:T(8,128)S(1)} %get-tuple-element.35), channel_id=1, source_target_pairs={{0,1},{2,3},{1,0},{3,2},{4,5},{6,7},{5,4},{7,6},{8,9},{10,11},{9,8... | collective-permute-start | bytes 602120 | tf_op jit(solution)/shard_map/ppermute | solution.py:574
  3.8 0.7 collective-permute-start
  4.5 2.5 %collective-permute-start.2 = (f32[392,128]{1,0:T(8,128)S(1)}, f32[392,128]{1,0:T(8,128)S(1)}, u32[]{:S(2)}, u32[]{:S(2)}) collective-permute-start(f32[392,128]{1,0:T(8,128)S(1)} %get-tuple-element.40), channel_id=1, source_target_pairs={{4,8},{12,16},{20,24},{8,4},{16,12},{24,20},{5,9},{13,17},{21,25},... | collective-permute-start | bytes 602120 | tf_op jit(solution)/shard_map/ppermute | solution.py:574
  7.0 1.1 %collective-permute-start.3 = (f32[392,128]{1,0:T(8,128)S(1)}, f32[392,128]{1,0:T(8,128)S(1)}, u32[]{:S(2)}, u32[]{:S(2)}) collective-permute-start(f32[392,128]{1,0:T(8,128)S(1)} %get-tuple-element.41), channel_id=1, source_target_pairs={{0,4},{8,12},{16,20},{24,28},{4,0},{12,8},{20,16},{28,24},{1,5},{9... | collective-permute-start | bytes 602120 | tf_op jit(solution)/shard_map/ppermute | solution.py:574
  8.1 1.3 %shard_map.65 = (f32[2,128,128]{2,1,0:T(8,128)S(1)}, f32[1,1,12,128,128]{4,3,2,1,0:T(8,128)S(1)}, bf16[4,256,256]{2,1,0:T(8,128)(2,1)S(1)}) custom-call(f32[392,128]{1,0:T(8,128)S(1)} %get-tuple-element.34.after.mine, f32[2,128,128]{2,1,0:T(8,128)} %probe_from.1, f32[1,1,12,128,128]{4,3,2,1,0:T(8,128)} %amps_from.1, ...), custom_call_target="tpu_custom_call" | custom-call | flops 201326592 | bytes 8000000 | tf_op jit(solution)/shard_map/pallas_call | solution.py:607
  9.4 0.1 shard_map.66
  9.5 3.0 %collective-permute-start.4 = (f32[136,128]{1,0:T(8,128)S(1)}, f32[136,128]{1,0:T(8,128)S(1)}, u32[]{:S(2)}, u32[]{:S(2)}) collective-permute-start(f32[136,128]{1,0:T(8,128)S(1)} %get-tuple-element.42), channel_id=1, source_target_pairs={{4,8},{12,16},{20,24},{8,4},{16,12},{24,20},{5,9},{13,17},{21,25},... | collective-permute-start | bytes 208904 | tf_op jit(solution)/shard_map/ppermute | solution.py:574
  12.5 0.2 collective-permute-start.5
  12.7 2.6 %shard_map.67.done = f32[2,3,384,128]{3,2,1,0:T(8,128)S(1)} custom-call(s32[1,1,2,12]{3,2,1,0:T(2,128)S(1)} %bitcast.2, s32[1,1]{1,0:T(1,128)S(6)} %copy.7.counts, f32[136,128]{1,0:T(8,128)S(1)} %get-tuple-element.37.after, f32[2,3,384,128]{3,2,1,0:T(8,128)S(1)} %get-tuple-element.33.field, f32[2,128,128]{2,1,0:T(8,128)S(1)} %get-tuple-element.36.after.probe, ...), custom_call_target="tpu_custom_call" | custom-call | flops 805306368 | bytes 8000000 | tf_op jit(solution)/shard_map/pallas_call | solution.py:621
  15.3 0.8 %collective-permute-done.4.corners_a = f32[136,128]{1,0:T(8,128)S(1)} collective-permute-done((f32[136,128]{1,0:T(8,128)S(1)}, f32[136,128]{1,0:T(8,128)S(1)}, u32[]{:S(2)}, u32[]{:S(2)}) %collective-permute-start.4) | collective-permute-done | bytes 69664 | tf_op jit(solution)/shard_map/ppermute | solution.py:574
  16.1 3.2 %shard_map.68 = (f32[2,5,512,128]{3,2,1,0:T(8,128)S(1)}, f32[2,5,512,128]{3,2,1,0:T(8,128)S(1)}, f32[2,2,128,128]{3,2,1,0:T(8,128)S(1)}, f32[2,2,128,128]{3,2,1,...) custom-call(s32[1,1,2,12]{3,2,1,0:T(2,128)S(1)} %bitcast.3, ...), custom_call_target="tpu_custom_call" | custom-call | tf_op jit(solution)/shard_map/pallas_call | solution.py:631
  19.3 2.5 %collective-permute-start.7 = (f32[2,2,128,128]{3,2,1,0:T(8,128)S(1)}, f32[2,2,128,128]{3,2,1,0:T(8,128)S(1)}, u32[]{:S(2)}, u32[]{:S(2)}) collective-permute-start(f32[2,2,128,128]{3,2,1,0:T(8,128)S(1)} %get-tuple-element.46.mine_b), channel_id=1, source_target_pairs={{0,1},{2,3},{1,0},{3,2},{4,5},{6,7},{5,4},{7,6},{8,9},{10,11},{9,8... | collective-permute-start | bytes 786440 | tf_op jit(solution)/shard_map/ppermute | solution.py:574
  21.8 0.7 collective-permute-start.8
  22.5 4.6 %collective-permute-start.6 = (f32[2,2,128,128]{3,2,1,0:T(8,128)S(1)}, f32[2,2,128,128]{3,2,1,0:T(8,128)S(1)}, u32[]{:S(2)}, u32[]{:S(2)}) collective-permute-start(f32[2,2,128,128]{3,2,1,0:T(8,128)S(1)} %get-tuple-element.43), channel_id=1, source_target_pairs={{4,8},{12,16},{20,24},{8,4},{16,12},{24,20},{5,9},{13,17},{21,25},... | collective-permute-start | bytes 786440 | tf_op jit(solution)/shard_map/ppermute | solution.py:574
  27.1 0.7 %collective-permute-start.9 = (f32[2,256,128]{2,1,0:T(8,128)S(1)}, f32[2,256,128]{2,1,0:T(8,128)S(1)}, u32[]{:S(2)}, u32[]{:S(2)}) collective-permute-start(f32[2,256,128]{2,1,0:T(8,128)S(1)} %get-tuple-element.48), channel_id=1, source_target_pairs={{1,2},{2,1},{5,6},{6,5},{9,10},{10,9},{13,14},{14,13},{17,18},{18,... | collective-permute-start | bytes 786440 | tf_op jit(solution)/shard_map/ppermute | solution.py:574
  27.8 4.6 %collective-permute-start.10 = (f32[2,256,128]{2,1,0:T(8,128)S(1)}, f32[2,256,128]{2,1,0:T(8,128)S(1)}, u32[]{:S(2)}, u32[]{:S(2)}) collective-permute-start(f32[2,256,128]{2,1,0:T(8,128)S(1)} %get-tuple-element.49), channel_id=1, source_target_pairs={{0,1},{2,3},{1,0},{3,2},{4,5},{6,7},{5,4},{7,6},{8,9},{10,11},{9,8... | collective-permute-start | bytes 786440 | tf_op jit(solution)/shard_map/ppermute | solution.py:574
  32.4 4.1 %collective-permute-start.12 = (f32[2,2,128,128]{3,2,1,0:T(8,128)S(1)}, f32[2,2,128,128]{3,2,1,0:T(8,128)S(1)}, u32[]{:S(2)}, u32[]{:S(2)}) collective-permute-start(f32[2,2,128,128]{3,2,1,0:T(8,128)S(1)} %shard_map.71), channel_id=1, source_target_pairs={{4,8},{12,16},{20,24},{8,4},{16,12},{24,20},{5,9},{13,17},{21,25},... | collective-permute-start | bytes 786440 | tf_op jit(solution)/shard_map/ppermute | solution.py:574
  36.5 3.3 %shard_map.69.inverse.after = f32[5,512,128]{2,1,0:T(8,128)S(1)} custom-call(f32[392,128]{1,0:T(8,128)S(1)} %get-tuple-element.34.after.mine, f32[392,128]{1,0:T(8,128)S(1)} %collective-permute-done.cols_a, f32[392,128]{1,0:T(8,128)S(1)} %collective-permute-done.1.cols_b, f32[392,128]{1,0:T(8,128)S(1)} %collective-permute-done.2.rows_a, ...), custom_call_target="tpu_custom_call" | custom-call | flops 1207959552 | bytes 8000000 | tf_op jit(solution)/shard_map/pallas_call | solution.py:640
  39.9 0.1 collective-permute-start.13
  40.0 7.0 %shard_map.70 = (f32[2,5,512,128]{3,2,1,0:T(8,128)S(1)}, f32[2,5,512,128]{3,2,1,0:T(8,128)S(1)}) custom-call(s32[1,1,2,12]{3,2,1,0:T(2,128)S(1)} %bitcast.4, s32[1,1]{1,0:T(1,128)S(6)} %copy.7.counts, f32[2,2,128,128]{3,2,1,0:T(8,128)S(1)} %collective-permute-done.6.after.edges_a, f32[2,5,512,128]{3,2,1,0:T(8,128)S(1)} %get-tuple-element.44.frame, ...), custom_call_target="tpu_custom_call" | custom-call | flops 1207959552 | bytes 8000000 | tf_op jit(solution)/shard_map/pallas_call | solution.py:655
  47.0 3.1 %shard_map.73 = (f32[2,5,512,128]{3,2,1,0:T(8,128)S(1)}, f32[2,3,384,128]{3,2,1,0:T(8,128)S(1)}, f32[512,128]{1,0:T(8,128)S(1)}, f32[512,128]{1,0:T(8,128)S(1)},...) custom-call(s32[1,1,2,12]{3,2,1,0:T(2,128)S(1)} %bitcast.5, s32[1,1]{1,0:T(1,128)S(6)} %copy.7.counts, ...), custom_call_target="tpu_custom_call" | custom-call | flops 1207959552 | bytes 8000000 | tf_op jit(solution)/shard_map/pallas_call | solution.py:661
  50.1 0.7 %collective-permute-start.14 = (f32[512,128]{1,0:T(8,128)S(1)}, f32[512,128]{1,0:T(8,128)S(1)}, u32[]{:S(2)}, u32[]{:S(2)}) collective-permute-start(f32[512,128]{1,0:T(8,128)S(1)} %get-tuple-element.55), channel_id=1, source_target_pairs={{1,2},{2,1},{5,6},{6,5},{9,10},{10,9},{13,14},{14,13},{17,18},{18,... | collective-permute-start | bytes 786440 | tf_op jit(solution)/shard_map/ppermute | solution.py:574
  50.8 0.1 collective-permute-start.15
  50.8 1.9 %collective-permute-start.16 = (f32[2,3,64,128]{3,2,1,0:T(8,128)S(1)}, f32[2,3,64,128]{3,2,1,0:T(8,128)S(1)}, u32[]{:S(2)}, u32[]{:S(2)}) collective-permute-start(f32[2,3,64,128]{3,2,1,0:T(8,128)S(1)} %get-tuple-element.57), channel_id=1, source_target_pairs={{4,8},{12,16},{20,24},{8,4},{16,12},{24,20},{5,9},{13,17},{21,25},... | collective-permute-start | bytes 589832 | tf_op jit(solution)/shard_map/ppermute | solution.py:574
  52.8 0.5 collective-permute-start.17
  53.3 6.2 %collective-permute-done.15.cols_b = f32[512,128]{1,0:T(8,128)S(1)} collective-permute-done((f32[512,128]{1,0:T(8,128)S(1)}, f32[512,128]{1,0:T(8,128)S(1)}, u32[]{:S(2)}, u32[]{:S(2)}) %collective-permute-start.15) | collective-permute-done | bytes 262176 | tf_op jit(solution)/shard_map/ppermute | solution.py:574
  59.5 1.9 %collective-permute-start.18 = (f32[2,64,128]{2,1,0:T(8,128)S(1)}, f32[2,64,128]{2,1,0:T(8,128)S(1)}, u32[]{:S(2)}, u32[]{:S(2)}) collective-permute-start(f32[2,64,128]{2,1,0:T(8,128)S(1)} %get-tuple-element.59), channel_id=1, source_target_pairs={{4,8},{12,16},{20,24},{8,4},{16,12},{24,20},{5,9},{13,17},{21,25},... | collective-permute-start | bytes 196616 | tf_op jit(solution)/shard_map/ppermute | solution.py:574
  61.5 0.1 collective-permute-start.19
  61.5 2.4 %shard_map.74.inner = f32[2,3,384,128]{3,2,1,0:T(8,128)S(1)} custom-call(s32[1,1,2,12]{3,2,1,0:T(2,128)S(1)} %bitcast.6, s32[1,1]{1,0:T(1,128)S(6)} %copy.7.counts, f32[2,5,512,128]{3,2,1,0:T(8,128)S(1)} %get-tuple-element.53.work, f32[2,128,128]{2,1,0:T(8,128)S(1)} %get-tuple-element.36.after.probe, f32[1,1,12,128,128]{4,3,2,1,0:T(8,128)S(1)} %get-tuple-element.38.amps, ...), custom_call_target="tpu_custom_call" | custom-call | flops 603979776 | bytes 8000000 | tf_op jit(solution)/shard_map/pallas_call | solution.py:668
  64.0 2.0 %collective-permute-done.18.corners_a = f32[2,64,128]{2,1,0:T(8,128)S(1)} collective-permute-done((f32[2,64,128]{2,1,0:T(8,128)S(1)}, f32[2,64,128]{2,1,0:T(8,128)S(1)}, u32[]{:S(2)}, u32[]{:S(2)}) %collective-permute-start.18) | collective-permute-done | bytes 65568 | tf_op jit(solution)/shard_map/ppermute | solution.py:574
  66.0 1.2 %shard_map.76 = f32[2,384,384]{2,1,0:T(8,128)} custom-call(f32[2,5,512,128]{3,2,1,0:T(8,128)S(1)} %get-tuple-element.53.work, f32[2,3,384,128]{3,2,1,0:T(8,128)S(1)} %get-tuple-element.54.sums, f32[2,3,384,128]{3,2,1,0:T(8,128)S(1)} %shard_map.74.inner, f32[5,512,128]{2,1,0:T(8,128)S(1)} %shard_map.69.inverse.after, ...), custom_call_target="tpu_custom_call" | custom-call | tf_op jit(solution)/shard_map/pallas_call | solution.py:673
  (23 shorter events, 0.2 us)
Async XLA Ops:
  2.1 10.5 %copy-start = (s32[1,1,12,2]{2,3,1,0:T(2,128)S(1)}, s32[1,1,12,2]{2,3,1,0:T(2,128)}, u32[]{:S(2)}) copy-start(s32[1,1,12,2]{2,3,1,0:T(2,128)} %param.9) | copy-start | bytes 292
  2.2 7.2 %collective-permute-start.1 = (f32[392,128]{1,0:T(8,128)S(1)}, f32[392,128]{1,0:T(8,128)S(1)}, u32[]{:S(2)}, u32[]{:S(2)}) collective-permute-start(f32[392,128]{1,0:T(8,128)S(1)} %get-tuple-element.35), channel_id=1, source_target_pairs={{0,1},{2,3},{1,0},{3,2},{4,5},{6,7},{5,4},{7,6},{8,9},{10,11},{9,8... | collective-permute-start | bytes 602120 | tf_op jit(solution)/shard_map/ppermute | solution.py:574
  3.8 5.6 %collective-permute-start = (f32[392,128]{1,0:T(8,128)S(1)}, f32[392,128]{1,0:T(8,128)S(1)}, u32[]{:S(2)}, u32[]{:S(2)}) collective-permute-start(f32[392,128]{1,0:T(8,128)S(1)} %get-tuple-element.34.after.mine), channel_id=1, source_target_pairs={{1,2},{2,1},{5,6},{6,5},{9,10},{10,9},{13,14},{14,13},{17,18},{18,... | collective-permute-start | bytes 602120 | tf_op jit(solution)/shard_map/ppermute | solution.py:574
  4.5 10.8 %collective-permute-start.2 = (f32[392,128]{1,0:T(8,128)S(1)}, f32[392,128]{1,0:T(8,128)S(1)}, u32[]{:S(2)}, u32[]{:S(2)}) collective-permute-start(f32[392,128]{1,0:T(8,128)S(1)} %get-tuple-element.40), channel_id=1, source_target_pairs={{4,8},{12,16},{20,24},{8,4},{16,12},{24,20},{5,9},{13,17},{21,25},... | collective-permute-start | bytes 602120 | tf_op jit(solution)/shard_map/ppermute | solution.py:574
  7.0 8.3 %collective-permute-start.3 = (f32[392,128]{1,0:T(8,128)S(1)}, f32[392,128]{1,0:T(8,128)S(1)}, u32[]{:S(2)}, u32[]{:S(2)}) collective-permute-start(f32[392,128]{1,0:T(8,128)S(1)} %get-tuple-element.41), channel_id=1, source_target_pairs={{0,4},{8,12},{16,20},{24,28},{4,0},{12,8},{20,16},{28,24},{1,5},{9... | collective-permute-start | bytes 602120 | tf_op jit(solution)/shard_map/ppermute | solution.py:574
  9.5 6.5 %collective-permute-start.4 = (f32[136,128]{1,0:T(8,128)S(1)}, f32[136,128]{1,0:T(8,128)S(1)}, u32[]{:S(2)}, u32[]{:S(2)}) collective-permute-start(f32[136,128]{1,0:T(8,128)S(1)} %get-tuple-element.42), channel_id=1, source_target_pairs={{4,8},{12,16},{20,24},{8,4},{16,12},{24,20},{5,9},{13,17},{21,25},... | collective-permute-start | bytes 208904 | tf_op jit(solution)/shard_map/ppermute | solution.py:574
  12.5 3.6 %collective-permute-start.5 = (f32[136,128]{1,0:T(8,128)S(1)}, f32[136,128]{1,0:T(8,128)S(1)}, u32[]{:S(2)}, u32[]{:S(2)}) collective-permute-start(f32[136,128]{1,0:T(8,128)S(1)} %get-tuple-element.37.after), channel_id=1, source_target_pairs={{0,4},{8,12},{16,20},{24,28},{4,0},{12,8},{20,16},{28,24},{1,5},{9... | collective-permute-start | bytes 208904 | tf_op jit(solution)/shard_map/ppermute | solution.py:574
  19.3 13.0 %collective-permute-start.7 = (f32[2,2,128,128]{3,2,1,0:T(8,128)S(1)}, f32[2,2,128,128]{3,2,1,0:T(8,128)S(1)}, u32[]{:S(2)}, u32[]{:S(2)}) collective-permute-start(f32[2,2,128,128]{3,2,1,0:T(8,128)S(1)} %get-tuple-element.46.mine_b), channel_id=1, source_target_pairs={{0,1},{2,3},{1,0},{3,2},{4,5},{6,7},{5,4},{7,6},{8,9},{10,11},{9,8... | collective-permute-start | bytes 786440 | tf_op jit(solution)/shard_map/ppermute | solution.py:574
  21.8 10.6 %collective-permute-start.8 = (f32[2,2,128,128]{3,2,1,0:T(8,128)S(1)}, f32[2,2,128,128]{3,2,1,0:T(8,128)S(1)}, u32[]{:S(2)}, u32[]{:S(2)}) collective-permute-start(f32[2,2,128,128]{3,2,1,0:T(8,128)S(1)} %get-tuple-element.47.mine_a), channel_id=1, source_target_pairs={{1,2},{2,1},{5,6},{6,5},{9,10},{10,9},{13,14},{14,13},{17,18},{18,... | collective-permute-start | bytes 786440 | tf_op jit(solution)/shard_map/ppermute | solution.py:574
  22.5 17.4 %collective-permute-start.6 = (f32[2,2,128,128]{3,2,1,0:T(8,128)S(1)}, f32[2,2,128,128]{3,2,1,0:T(8,128)S(1)}, u32[]{:S(2)}, u32[]{:S(2)}) collective-permute-start(f32[2,2,128,128]{3,2,1,0:T(8,128)S(1)} %get-tuple-element.43), channel_id=1, source_target_pairs={{4,8},{12,16},{20,24},{8,4},{16,12},{24,20},{5,9},{13,17},{21,25},... | collective-permute-start | bytes 786440 | tf_op jit(solution)/shard_map/ppermute | solution.py:574
  27.1 12.9 %collective-permute-start.9 = (f32[2,256,128]{2,1,0:T(8,128)S(1)}, f32[2,256,128]{2,1,0:T(8,128)S(1)}, u32[]{:S(2)}, u32[]{:S(2)}) collective-permute-start(f32[2,256,128]{2,1,0:T(8,128)S(1)} %get-tuple-element.48), channel_id=1, source_target_pairs={{1,2},{2,1},{5,6},{6,5},{9,10},{10,9},{13,14},{14,13},{17,18},{18,... | collective-permute-start | bytes 786440 | tf_op jit(solution)/shard_map/ppermute | solution.py:574
  27.8 12.2 %collective-permute-start.10 = (f32[2,256,128]{2,1,0:T(8,128)S(1)}, f32[2,256,128]{2,1,0:T(8,128)S(1)}, u32[]{:S(2)}, u32[]{:S(2)}) collective-permute-start(f32[2,256,128]{2,1,0:T(8,128)S(1)} %get-tuple-element.49), channel_id=1, source_target_pairs={{0,1},{2,3},{1,0},{3,2},{4,5},{6,7},{5,4},{7,6},{8,9},{10,11},{9,8... | collective-permute-start | bytes 786440 | tf_op jit(solution)/shard_map/ppermute | solution.py:574
  32.3 14.6 %collective-permute-start.11 = (f32[2,2,128,128]{3,2,1,0:T(8,128)S(1)}, f32[2,2,128,128]{3,2,1,0:T(8,128)S(1)}, u32[]{:S(2)}, u32[]{:S(2)}) collective-permute-start(f32[2,2,128,128]{3,2,1,0:T(8,128)S(1)} %get-tuple-element.52), channel_id=1, source_target_pairs={{0,4},{8,12},{16,20},{24,28},{4,0},{12,8},{20,16},{28,24},{1,5},{9... | collective-permute-start | bytes 786440 | tf_op jit(solution)/shard_map/ppermute | solution.py:574
  32.4 14.5 %collective-permute-start.12 = (f32[2,2,128,128]{3,2,1,0:T(8,128)S(1)}, f32[2,2,128,128]{3,2,1,0:T(8,128)S(1)}, u32[]{:S(2)}, u32[]{:S(2)}) collective-permute-start(f32[2,2,128,128]{3,2,1,0:T(8,128)S(1)} %shard_map.71), channel_id=1, source_target_pairs={{4,8},{12,16},{20,24},{8,4},{16,12},{24,20},{5,9},{13,17},{21,25},... | collective-permute-start | bytes 786440 | tf_op jit(solution)/shard_map/ppermute | solution.py:574
  39.9 7.1 %collective-permute-start.13 = (f32[2,2,128,128]{3,2,1,0:T(8,128)S(1)}, f32[2,2,128,128]{3,2,1,0:T(8,128)S(1)}, u32[]{:S(2)}, u32[]{:S(2)}) collective-permute-start(f32[2,2,128,128]{3,2,1,0:T(8,128)S(1)} %shard_map.72), channel_id=1, source_target_pairs={{0,4},{8,12},{16,20},{24,28},{4,0},{12,8},{20,16},{28,24},{1,5},{9... | collective-permute-start | bytes 786440 | tf_op jit(solution)/shard_map/ppermute | solution.py:574
  50.1 3.2 %collective-permute-start.14 = (f32[512,128]{1,0:T(8,128)S(1)}, f32[512,128]{1,0:T(8,128)S(1)}, u32[]{:S(2)}, u32[]{:S(2)}) collective-permute-start(f32[512,128]{1,0:T(8,128)S(1)} %get-tuple-element.55), channel_id=1, source_target_pairs={{1,2},{2,1},{5,6},{6,5},{9,10},{10,9},{13,14},{14,13},{17,18},{18,... | collective-permute-start | bytes 786440 | tf_op jit(solution)/shard_map/ppermute | solution.py:574
  50.8 8.7 %collective-permute-start.15 = (f32[512,128]{1,0:T(8,128)S(1)}, f32[512,128]{1,0:T(8,128)S(1)}, u32[]{:S(2)}, u32[]{:S(2)}) collective-permute-start(f32[512,128]{1,0:T(8,128)S(1)} %get-tuple-element.56), channel_id=1, source_target_pairs={{0,1},{2,3},{1,0},{3,2},{4,5},{6,7},{5,4},{7,6},{8,9},{10,11},{9,8... | collective-permute-start | bytes 786440 | tf_op jit(solution)/shard_map/ppermute | solution.py:574
  50.8 13.1 %collective-permute-start.16 = (f32[2,3,64,128]{3,2,1,0:T(8,128)S(1)}, f32[2,3,64,128]{3,2,1,0:T(8,128)S(1)}, u32[]{:S(2)}, u32[]{:S(2)}) collective-permute-start(f32[2,3,64,128]{3,2,1,0:T(8,128)S(1)} %get-tuple-element.57), channel_id=1, source_target_pairs={{4,8},{12,16},{20,24},{8,4},{16,12},{24,20},{5,9},{13,17},{21,25},... | collective-permute-start | bytes 589832 | tf_op jit(solution)/shard_map/ppermute | solution.py:574
  52.8 11.2 %collective-permute-start.17 = (f32[2,3,64,128]{3,2,1,0:T(8,128)S(1)}, f32[2,3,64,128]{3,2,1,0:T(8,128)S(1)}, u32[]{:S(2)}, u32[]{:S(2)}) collective-permute-start(f32[2,3,64,128]{3,2,1,0:T(8,128)S(1)} %get-tuple-element.58), channel_id=1, source_target_pairs={{0,4},{8,12},{16,20},{24,28},{4,0},{12,8},{20,16},{28,24},{1,5},{9... | collective-permute-start | bytes 589832 | tf_op jit(solution)/shard_map/ppermute | solution.py:574
  59.5 6.5 %collective-permute-start.18 = (f32[2,64,128]{2,1,0:T(8,128)S(1)}, f32[2,64,128]{2,1,0:T(8,128)S(1)}, u32[]{:S(2)}, u32[]{:S(2)}) collective-permute-start(f32[2,64,128]{2,1,0:T(8,128)S(1)} %get-tuple-element.59), channel_id=1, source_target_pairs={{4,8},{12,16},{20,24},{8,4},{16,12},{24,20},{5,9},{13,17},{21,25},... | collective-permute-start | bytes 196616 | tf_op jit(solution)/shard_map/ppermute | solution.py:574
  61.5 4.6 %collective-permute-start.19 = (f32[2,64,128]{2,1,0:T(8,128)S(1)}, f32[2,64,128]{2,1,0:T(8,128)S(1)}, u32[]{:S(2)}, u32[]{:S(2)}) collective-permute-start(f32[2,64,128]{2,1,0:T(8,128)S(1)} %get-tuple-element.60), channel_id=1, source_target_pairs={{0,4},{8,12},{16,20},{24,28},{4,0},{12,8},{20,16},{28,24},{1,5},{9... | collective-permute-start | bytes 196616 | tf_op jit(solution)/shard_map/ppermute | solution.py:574
where the time goes:
time: 68.4 us; the launch traced here: 67.2 us
  starting transfers between devices  31.3 us (46%)
  Pallas kernels  25.9 us (38%)
  waiting for transfers between devices  9.04 us (13%)
  between operations  0.95 us (1%)
    ppermute x20, starting transfers between devices, swap_pairs(): got.append(lax.ppermute(value, axis, pairs + [(b, a) for a, b in pairs]))  31.3 us
    ppermute x20, waiting for transfers between devices, swap_pairs(): got.append(lax.ppermute(value, axis, pairs + [(b, a) for a, b in pairs]))  9.04 us
    pallas_call x1, Pallas kernels, shards(): call(update_pass, [full, full], 'ssa' + 10 * 'v', [chosen], cost(npos // 2))  6.96 us
    pallas_call x1, Pallas kernels, shards(): call(functools.partial(light_pass, npos=npos), [(blocks, rows, length)],...  3.31 us
    pallas_call x1, Pallas kernels, shards(): call(first_pass, [full, full, tip, tip, strip, strip, edge, edge], 'ss' +...  3.24 us
    pallas_call x1, Pallas kernels, shards(): call(second_pass, [full, own, strip, strip, edge, edge], 'ss' + 10 * 'v',...  3.08 us
    pallas_call x1, Pallas kernels, shards(): call(early_pass, [(2, nb, tile, length)], 'ssavvvv', [chosen], cost(GROUP))  2.62 us
    pallas_call x1, Pallas kernels, shards(): call(inner_pass, [own], 'ss' + 4 * 'v', [chosen], cost(npos // 4))  2.4 us
  transfers between devices with their start and end apart: 20, of which 3 were waited for; matrix products, arithmetic and copies ran while one was open for 0% of the time, Pallas kernels for 25%

commit v1 on v0

--- a/solution.py
+++ b/solution.py
@@ -125,7 +125,7 @@
     found, _ = collect(chosen, 0, *place, touching)
     found, known = collect(chosen, found, *place, early, GROUP)
     begin = GROUP - jnp.minimum(known, GROUP)
-    end = begin + lax.rem(GROUP - lax.rem(found, GROUP), GROUP)
+    end = begin + lax.rem(CHAIN - lax.rem(found, CHAIN), CHAIN)
     found, _ = collect(chosen, found, *place, clear, begin, end)
     return found, end
 
@@ -216,19 +216,27 @@
             for k in range(len(slots))
         ]
 
-    def step(index, carry):
-        places = [index * GROUP + k for k in range(GROUP)]
+    def run(first, count):
+        places = [first + k for k in range(count)]
         slots = [chosen[jnp.where(at < found, at, 0)] for at in places]
-        chains = [work(slots[k:k + CHAIN]) for k in range(0, GROUP, CHAIN)]
+        chains = [work(slots[k:k + CHAIN]) for k in range(0, count, CHAIN)]
         gradients = [None]
         while gradients[0] is None:
             gradients = [next(chain) for chain in chains]
         gradients = [gradient for chain in gradients for gradient in chain]
         for at, slot, gradient in zip(places, slots, gradients):
             put(slot, at < found, *gradient)
+
+    def step(index, carry):
+        run(index * GROUP, GROUP)
         return carry
 
-    lax.fori_loop(0, (found + GROUP - 1) // GROUP, step, 0)
+    steps = lax.div(found + GROUP - CHAIN - 1, GROUP)
+    lax.fori_loop(0, steps, step, 0)
+
+    @pl.when(found > steps * GROUP)
+    def _():
+        run(steps * GROUP, CHAIN)
 
 
 def start_pass(field, offsets_from, counts, tile_out, cols_a, cols_b, rows_a, rows_b, offsets, sems):
@@ -464,7 +472,7 @@
 
 def second_pass(offsets, counts, work_from, total_from, inverse, edges_a, edges_b,
                 corners_a, corners_b, probe, amps, tables,
-                work, sums, cols_a, cols_b, rows_a, rows_b, total, chosen):
+                work, total, cols_a, cols_b, rows_a, rows_b, chosen):
     _, blocks, rows, length = work.shape
     half = length // 2
     nb = blocks - 2
@@ -496,7 +504,6 @@
     )
     for part in (0, 1):
         for b in range(nb):
-            sums[part, b] = total[part, b + 1, pl.ds(half, tile), :]
             rows_a[part, b], rows_b[part, b] = by_pairs(
                 "row", total[part, b + 1, :half, :], total[part, b + 1, half + tile:, :])
 
@@ -517,9 +524,9 @@
         corners_a[side], corners_b[side] = by_pairs("row", value[:half], value[rows - half:])
 
 
-def last_pass(work, sums, inner, inverse, cols_a, cols_b, rows_a, rows_b, corners_a, corners_b,
+def last_pass(work, total, inner, inverse, cols_a, cols_b, rows_a, rows_b, corners_a, corners_b,
               out, result, sems):
-    _, nb, tile, length = sums.shape
+    _, nb, tile, length = inner.shape
     half = length // 2
     low = lanes((tile, length)) < half
     own = pl.ds(half, tile)
@@ -535,7 +542,7 @@
             left, right = swap(left, half), swap(right, half)
         for b in range(nb):
             up, down = by_side("row", rows_a[part, b], rows_b[part, b])
-            value = sums[part, b] + inner[part, b] + above(above(up, gap), down)
+            value = total[part, b + 1, own, :] + inner[part, b] + above(above(up, gap), down)
             if b == 0:
                 value = value + jnp.where(low, left, 0.0)
             if b == nb - 1:
@@ -658,9 +665,9 @@
     strip = (rows, length)
     own = (2, nb, tile, length)
     edge = (2, nb, half, length)
-    work, sums, cols_a, cols_b, rows_a, rows_b = call(
-        second_pass, [full, own, strip, strip, edge, edge], "ss" + 10 * "v",
-        [memory(full, jnp.float32), chosen], cost(npos // 2),
+    work, total, cols_a, cols_b, rows_a, rows_b = call(
+        second_pass, [full, full, strip, strip, edge, edge], "ss" + 10 * "v",
+        [chosen], cost(npos // 2),
     )(offsets, counts, work, total, inverse, edges_a, edges_b, corners_a, corners_b,
       probe, amplitudes, tables)
     cols_a, cols_b = swap_pairs(cols_a, cols_b, "col")
@@ -677,7 +684,7 @@
         out_specs=whole(pl.ANY),
         scratch_shapes=[memory(own, jnp.float32), pltpu.SemaphoreType.DMA((2 * nb,))],
         compiler_params=pltpu.CompilerParams(vmem_limit_bytes=VMEM_BYTES),
-    )(work, sums, inner, inverse, cols_a, cols_b, rows_a, rows_b, corners_a, corners_b)
+    )(work, total, inner, inverse, cols_a, cols_b, rows_a, rows_b, corners_a, corners_b)
     return out
 
 

time: 68.4 us -> 68.8 us (level)
  the two profiles are of different devices: /device:TPU:4 before, /device:TPU:1 now
where the time goes in v1:
time: 68.8 us; the launch traced here: 68.2 us
  starting transfers between devices  33.7 us (49%)
  Pallas kernels  28 us (41%)
  waiting for transfers between devices  5.35 us (8%)
  between operations  1.16 us (2%)
    ppermute x20, starting transfers between devices, swap_pairs(): got.append(lax.ppermute(value, axis, pairs + [(b, a) for a, b in pairs]))  33.7 us
    pallas_call x1, Pallas kernels, shards(): call(first_pass, [full, full, tip, tip, strip, strip, edge, edge], 'ss' +...  6.29 us
    ppermute x20, waiting for transfers between devices, swap_pairs(): got.append(lax.ppermute(value, axis, pairs + [(b, a) for a, b in pairs]))  5.35 us
    pallas_call x1, Pallas kernels, shards(): call(second_pass, [full, full, strip, strip, edge, edge], 'ss' + 10 * 'v'...  4.62 us
    pallas_call x1, Pallas kernels, shards(): call(functools.partial(light_pass, npos=npos), [(blocks, rows, length)],...  4.15 us
    pallas_call x1, Pallas kernels, shards(): call(update_pass, [full, full], 'ssa' + 10 * 'v', [chosen], cost(npos // 2))  3.96 us
    pallas_call x1, Pallas kernels, shards(): call(early_pass, [(2, nb, tile, length)], 'ssavvvv', [chosen], cost(GROUP))  2.43 us
    pallas_call x1, Pallas kernels, shards(): call(inner_pass, [own], 'ss' + 4 * 'v', [chosen], cost(npos // 4))  2.23 us
  transfers between devices with their start and end apart: 20, of which 2 were waited for; matrix products, arithmetic and copies ran while one was open for 0% of the time, Pallas kernels for 21%

profile of v1, /device:TPU:1, one launch (start us, length us, event | category | flops | bytes accessed | tf_op | source)
XLA Modules:
  0.0 68.2 jit_solution(15155061418369444906)
XLA Ops:
  0.7 1.5 %shard_map.64 = (f32[2,3,384,128]{3,2,1,0:T(8,128)S(1)}, f32[392,128]{1,0:T(8,128)S(1)}, f32[392,128]{1,0:T(8,128)S(1)}, f32[392,128]{1,0:T(8,128)S(1)}, f32[392,128]{1,0:T(8,128)S(1)}) custom-call(f32[2,384,384]{2,1,0:T(8,128)} %field.1, s32[1,1,2,12]{3,2,1,0:T(2,128)} %bitcast.1, s32[1,1]{1,0:T(1,128)S(6)} %copy.7.counts), custom_call_target="tpu_custom_call" | custom-call | tf_op jit(solution)/shard_map/pallas_call | solution.py:609
  2.2 2.2 %collective-permute-start.1 = (f32[392,128]{1,0:T(8,128)S(1)}, f32[392,128]{1,0:T(8,128)S(1)}, u32[]{:S(2)}, u32[]{:S(2)}) collective-permute-start(f32[392,128]{1,0:T(8,128)S(1)} %get-tuple-element.35), channel_id=1, source_target_pairs={{0,1},{2,3},{1,0},{3,2},{4,5},{6,7},{5,4},{7,6},{8,9},{10,11},{9,8... | collective-permute-start | bytes 602120 | tf_op jit(solution)/shard_map/ppermute | solution.py:581
  4.4 0.7 collective-permute-start
  5.0 4.0 %collective-permute-start.2 = (f32[392,128]{1,0:T(8,128)S(1)}, f32[392,128]{1,0:T(8,128)S(1)}, u32[]{:S(2)}, u32[]{:S(2)}) collective-permute-start(f32[392,128]{1,0:T(8,128)S(1)} %get-tuple-element.40), channel_id=1, source_target_pairs={{4,8},{12,16},{20,24},{8,4},{16,12},{24,20},{5,9},{13,17},{21,25},... | collective-permute-start | bytes 602120 | tf_op jit(solution)/shard_map/ppermute | solution.py:581
  9.0 0.1 collective-permute-start.3
  9.1 1.3 %shard_map.65 = (f32[2,128,128]{2,1,0:T(8,128)S(1)}, f32[1,1,12,128,128]{4,3,2,1,0:T(8,128)S(1)}, bf16[4,256,256]{2,1,0:T(8,128)(2,1)S(1)}) custom-call(f32[392,128]{1,0:T(8,128)S(1)} %get-tuple-element.34.after.mine, f32[2,128,128]{2,1,0:T(8,128)} %probe_from.1, f32[1,1,12,128,128]{4,3,2,1,0:T(8,128)} %amps_from.1, ...), custom_call_target="tpu_custom_call" | custom-call | flops 201326592 | bytes 8000000 | tf_op jit(solution)/shard_map/pallas_call | solution.py:614
  10.4 0.1 shard_map.66
  10.5 3.5 %collective-permute-start.4 = (f32[136,128]{1,0:T(8,128)S(1)}, f32[136,128]{1,0:T(8,128)S(1)}, u32[]{:S(2)}, u32[]{:S(2)}) collective-permute-start(f32[136,128]{1,0:T(8,128)S(1)} %get-tuple-element.42), channel_id=1, source_target_pairs={{4,8},{12,16},{20,24},{8,4},{16,12},{24,20},{5,9},{13,17},{21,25},... | collective-permute-start | bytes 208904 | tf_op jit(solution)/shard_map/ppermute | solution.py:581
  14.1 0.1 collective-permute-start.5
  14.1 2.4 %shard_map.67.done = f32[2,3,384,128]{3,2,1,0:T(8,128)S(1)} custom-call(s32[1,1,2,12]{3,2,1,0:T(2,128)S(1)} %bitcast.2, s32[1,1]{1,0:T(1,128)S(6)} %copy.7.counts, f32[136,128]{1,0:T(8,128)S(1)} %get-tuple-element.37.after, f32[2,3,384,128]{3,2,1,0:T(8,128)S(1)} %get-tuple-element.33.field, f32[2,128,128]{2,1,0:T(8,128)S(1)} %get-tuple-element.36.after.probe, ...), custom_call_target="tpu_custom_call" | custom-call | flops 805306368 | bytes 8000000 | tf_op jit(solution)/shard_map/pallas_call | solution.py:628
  16.6 6.3 %shard_map.68 = (f32[2,5,512,128]{3,2,1,0:T(8,128)S(1)}, f32[2,5,512,128]{3,2,1,0:T(8,128)S(1)}, f32[2,2,128,128]{3,2,1,0:T(8,128)S(1)}, f32[2,2,128,128]{3,2,1,...) custom-call(s32[1,1,2,12]{3,2,1,0:T(2,128)S(1)} %bitcast.3, ...), custom_call_target="tpu_custom_call" | custom-call | tf_op jit(solution)/shard_map/pallas_call | solution.py:638
  22.9 4.2 %collective-permute-start.7 = (f32[2,2,128,128]{3,2,1,0:T(8,128)S(1)}, f32[2,2,128,128]{3,2,1,0:T(8,128)S(1)}, u32[]{:S(2)}, u32[]{:S(2)}) collective-permute-start(f32[2,2,128,128]{3,2,1,0:T(8,128)S(1)} %get-tuple-element.46.mine_b), channel_id=1, source_target_pairs={{0,1},{2,3},{1,0},{3,2},{4,5},{6,7},{5,4},{7,6},{8,9},{10,11},{9,8... | collective-permute-start | bytes 786440 | tf_op jit(solution)/shard_map/ppermute | solution.py:581
  27.1 0.7 collective-permute-start.8
  27.8 1.9 %collective-permute-start.6 = (f32[2,2,128,128]{3,2,1,0:T(8,128)S(1)}, f32[2,2,128,128]{3,2,1,0:T(8,128)S(1)}, u32[]{:S(2)}, u32[]{:S(2)}) collective-permute-start(f32[2,2,128,128]{3,2,1,0:T(8,128)S(1)} %get-tuple-element.43), channel_id=1, source_target_pairs={{4,8},{12,16},{20,24},{8,4},{16,12},{24,20},{5,9},{13,17},{21,25},... | collective-permute-start | bytes 786440 | tf_op jit(solution)/shard_map/ppermute | solution.py:581
  29.7 0.7 collective-permute-start.9
  30.4 4.0 %collective-permute-start.10 = (f32[2,256,128]{2,1,0:T(8,128)S(1)}, f32[2,256,128]{2,1,0:T(8,128)S(1)}, u32[]{:S(2)}, u32[]{:S(2)}) collective-permute-start(f32[2,256,128]{2,1,0:T(8,128)S(1)} %get-tuple-element.49), channel_id=1, source_target_pairs={{0,1},{2,3},{1,0},{3,2},{4,5},{6,7},{5,4},{7,6},{8,9},{10,11},{9,8... | collective-permute-start | bytes 786440 | tf_op jit(solution)/shard_map/ppermute | solution.py:581
  34.4 0.1 shard_map.71
  34.5 4.2 %collective-permute-start.12 = (f32[2,2,128,128]{3,2,1,0:T(8,128)S(1)}, f32[2,2,128,128]{3,2,1,0:T(8,128)S(1)}, u32[]{:S(2)}, u32[]{:S(2)}) collective-permute-start(f32[2,2,128,128]{3,2,1,0:T(8,128)S(1)} %shard_map.71), channel_id=1, source_target_pairs={{4,8},{12,16},{20,24},{8,4},{16,12},{24,20},{5,9},{13,17},{21,25},... | collective-permute-start | bytes 786440 | tf_op jit(solution)/shard_map/ppermute | solution.py:581
  38.7 4.2 %shard_map.69.inverse.after = f32[5,512,128]{2,1,0:T(8,128)S(1)} custom-call(f32[392,128]{1,0:T(8,128)S(1)} %get-tuple-element.34.after.mine, f32[392,128]{1,0:T(8,128)S(1)} %collective-permute-done.cols_a, f32[392,128]{1,0:T(8,128)S(1)} %collective-permute-done.1.cols_b, f32[392,128]{1,0:T(8,128)S(1)} %collective-permute-done.2.rows_a, ...), custom_call_target="tpu_custom_call" | custom-call | flops 1207959552 | bytes 8000000 | tf_op jit(solution)/shard_map/pallas_call | solution.py:647
  42.9 0.1 shard_map.72
  43.0 0.1 collective-permute-start.13
  43.1 4.0 %shard_map.70 = (f32[2,5,512,128]{3,2,1,0:T(8,128)S(1)}, f32[2,5,512,128]{3,2,1,0:T(8,128)S(1)}) custom-call(s32[1,1,2,12]{3,2,1,0:T(2,128)S(1)} %bitcast.4, s32[1,1]{1,0:T(1,128)S(6)} %copy.7.counts, f32[2,2,128,128]{3,2,1,0:T(8,128)S(1)} %collective-permute-done.6.after.edges_a, f32[2,5,512,128]{3,2,1,0:T(8,128)S(1)} %get-tuple-element.44.frame, ...), custom_call_target="tpu_custom_call" | custom-call | flops 1207959552 | bytes 8000000 | tf_op jit(solution)/shard_map/pallas_call | solution.py:662
  47.1 4.6 %shard_map.73 = (f32[2,5,512,128]{3,2,1,0:T(8,128)S(1)}, f32[2,5,512,128]{3,2,1,0:T(8,128)S(1)}, f32[512,128]{1,0:T(8,128)S(1)}, f32[512,128]{1,0:T(8,128)S(1)},...) custom-call(s32[1,1,2,12]{3,2,1,0:T(2,128)S(1)} %bitcast.5, s32[1,1]{1,0:T(1,128)S(6)} %copy.7.counts, ...), custom_call_target="tpu_custom_call" | custom-call | flops 1207959552 | bytes 8000000 | tf_op jit(solution)/shard_map/pallas_call | solution.py:668
  51.7 0.7 collective-permute-start.14
  52.4 2.8 %collective-permute-start.15 = (f32[512,128]{1,0:T(8,128)S(1)}, f32[512,128]{1,0:T(8,128)S(1)}, u32[]{:S(2)}, u32[]{:S(2)}) collective-permute-start(f32[512,128]{1,0:T(8,128)S(1)} %get-tuple-element.56), channel_id=1, source_target_pairs={{0,1},{2,3},{1,0},{3,2},{4,5},{6,7},{5,4},{7,6},{8,9},{10,11},{9,8... | collective-permute-start | bytes 786440 | tf_op jit(solution)/shard_map/ppermute | solution.py:581
  55.2 1.9 %collective-permute-start.16 = (f32[2,3,64,128]{3,2,1,0:T(8,128)S(1)}, f32[2,3,64,128]{3,2,1,0:T(8,128)S(1)}, u32[]{:S(2)}, u32[]{:S(2)}) collective-permute-start(f32[2,3,64,128]{3,2,1,0:T(8,128)S(1)} %get-tuple-element.57), channel_id=1, source_target_pairs={{4,8},{12,16},{20,24},{8,4},{16,12},{24,20},{5,9},{13,17},{21,25},... | collective-permute-start | bytes 589832 | tf_op jit(solution)/shard_map/ppermute | solution.py:581
  57.2 4.0 %collective-permute-done.15.cols_b = f32[512,128]{1,0:T(8,128)S(1)} collective-permute-done((f32[512,128]{1,0:T(8,128)S(1)}, f32[512,128]{1,0:T(8,128)S(1)}, u32[]{:S(2)}, u32[]{:S(2)}) %collective-permute-start.15) | collective-permute-done | bytes 262176 | tf_op jit(solution)/shard_map/ppermute | solution.py:581
  61.2 1.9 %collective-permute-start.18 = (f32[2,64,128]{2,1,0:T(8,128)S(1)}, f32[2,64,128]{2,1,0:T(8,128)S(1)}, u32[]{:S(2)}, u32[]{:S(2)}) collective-permute-start(f32[2,64,128]{2,1,0:T(8,128)S(1)} %get-tuple-element.59), channel_id=1, source_target_pairs={{4,8},{12,16},{20,24},{8,4},{16,12},{24,20},{5,9},{13,17},{21,25},... | collective-permute-start | bytes 196616 | tf_op jit(solution)/shard_map/ppermute | solution.py:581
  63.2 0.1 collective-permute-start.19
  63.2 2.2 %shard_map.74.inner = f32[2,3,384,128]{3,2,1,0:T(8,128)S(1)} custom-call(s32[1,1,2,12]{3,2,1,0:T(2,128)S(1)} %bitcast.6, s32[1,1]{1,0:T(1,128)S(6)} %copy.7.counts, f32[2,5,512,128]{3,2,1,0:T(8,128)S(1)} %get-tuple-element.53.work, f32[2,128,128]{2,1,0:T(8,128)S(1)} %get-tuple-element.36.after.probe, f32[1,1,12,128,128]{4,3,2,1,0:T(8,128)S(1)} %get-tuple-element.38.amps, ...), custom_call_target="tpu_custom_call" | custom-call | flops 603979776 | bytes 8000000 | tf_op jit(solution)/shard_map/pallas_call | solution.py:675
  65.5 1.3 %collective-permute-done.18.corners_a = f32[2,64,128]{2,1,0:T(8,128)S(1)} collective-permute-done((f32[2,64,128]{2,1,0:T(8,128)S(1)}, f32[2,64,128]{2,1,0:T(8,128)S(1)}, u32[]{:S(2)}, u32[]{:S(2)}) %collective-permute-start.18) | collective-permute-done | bytes 65568 | tf_op jit(solution)/shard_map/ppermute | solution.py:581
  66.8 1.2 %shard_map.76 = f32[2,384,384]{2,1,0:T(8,128)} custom-call(f32[2,5,512,128]{3,2,1,0:T(8,128)S(1)} %get-tuple-element.53.work, f32[2,5,512,128]{3,2,1,0:T(8,128)S(1)} %get-tuple-element.54.total, f32[2,3,384,128]{3,2,1,0:T(8,128)S(1)} %shard_map.74.inner, f32[5,512,128]{2,1,0:T(8,128)S(1)} %shard_map.69.inverse.after, ...), custom_call_target="tpu_custom_call" | custom-call | tf_op jit(solution)/shard_map/pallas_call | solution.py:680
  (23 shorter events, 0.1 us)
Async XLA Ops:
  0.0 14.1 %copy-start = (s32[1,1,12,2]{2,3,1,0:T(2,128)S(1)}, s32[1,1,12,2]{2,3,1,0:T(2,128)}, u32[]{:S(2)}) copy-start(s32[1,1,12,2]{2,3,1,0:T(2,128)} %param.9) | copy-start | bytes 292
  2.2 8.2 %collective-permute-start.1 = (f32[392,128]{1,0:T(8,128)S(1)}, f32[392,128]{1,0:T(8,128)S(1)}, u32[]{:S(2)}, u32[]{:S(2)}) collective-permute-start(f32[392,128]{1,0:T(8,128)S(1)} %get-tuple-element.35), channel_id=1, source_target_pairs={{0,1},{2,3},{1,0},{3,2},{4,5},{6,7},{5,4},{7,6},{8,9},{10,11},{9,8... | collective-permute-start | bytes 602120 | tf_op jit(solution)/shard_map/ppermute | solution.py:581
  4.4 6.1 %collective-permute-start = (f32[392,128]{1,0:T(8,128)S(1)}, f32[392,128]{1,0:T(8,128)S(1)}, u32[]{:S(2)}, u32[]{:S(2)}) collective-permute-start(f32[392,128]{1,0:T(8,128)S(1)} %get-tuple-element.34.after.mine), channel_id=1, source_target_pairs={{1,2},{2,1},{5,6},{6,5},{9,10},{10,9},{13,14},{14,13},{17,18},{18,... | collective-permute-start | bytes 602120 | tf_op jit(solution)/shard_map/ppermute | solution.py:581
  5.0 11.6 %collective-permute-start.2 = (f32[392,128]{1,0:T(8,128)S(1)}, f32[392,128]{1,0:T(8,128)S(1)}, u32[]{:S(2)}, u32[]{:S(2)}) collective-permute-start(f32[392,128]{1,0:T(8,128)S(1)} %get-tuple-element.40), channel_id=1, source_target_pairs={{4,8},{12,16},{20,24},{8,4},{16,12},{24,20},{5,9},{13,17},{21,25},... | collective-permute-start | bytes 602120 | tf_op jit(solution)/shard_map/ppermute | solution.py:581
  9.0 7.6 %collective-permute-start.3 = (f32[392,128]{1,0:T(8,128)S(1)}, f32[392,128]{1,0:T(8,128)S(1)}, u32[]{:S(2)}, u32[]{:S(2)}) collective-permute-start(f32[392,128]{1,0:T(8,128)S(1)} %get-tuple-element.41), channel_id=1, source_target_pairs={{0,4},{8,12},{16,20},{24,28},{4,0},{12,8},{20,16},{28,24},{1,5},{9... | collective-permute-start | bytes 602120 | tf_op jit(solution)/shard_map/ppermute | solution.py:581
  10.5 6.1 %collective-permute-start.4 = (f32[136,128]{1,0:T(8,128)S(1)}, f32[136,128]{1,0:T(8,128)S(1)}, u32[]{:S(2)}, u32[]{:S(2)}) collective-permute-start(f32[136,128]{1,0:T(8,128)S(1)} %get-tuple-element.42), channel_id=1, source_target_pairs={{4,8},{12,16},{20,24},{8,4},{16,12},{24,20},{5,9},{13,17},{21,25},... | collective-permute-start | bytes 208904 | tf_op jit(solution)/shard_map/ppermute | solution.py:581
  14.1 2.6 %collective-permute-start.5 = (f32[136,128]{1,0:T(8,128)S(1)}, f32[136,128]{1,0:T(8,128)S(1)}, u32[]{:S(2)}, u32[]{:S(2)}) collective-permute-start(f32[136,128]{1,0:T(8,128)S(1)} %get-tuple-element.37.after), channel_id=1, source_target_pairs={{0,4},{8,12},{16,20},{24,28},{4,0},{12,8},{20,16},{28,24},{1,5},{9... | collective-permute-start | bytes 208904 | tf_op jit(solution)/shard_map/ppermute | solution.py:581
  22.9 11.5 %collective-permute-start.7 = (f32[2,2,128,128]{3,2,1,0:T(8,128)S(1)}, f32[2,2,128,128]{3,2,1,0:T(8,128)S(1)}, u32[]{:S(2)}, u32[]{:S(2)}) collective-permute-start(f32[2,2,128,128]{3,2,1,0:T(8,128)S(1)} %get-tuple-element.46.mine_b), channel_id=1, source_target_pairs={{0,1},{2,3},{1,0},{3,2},{4,5},{6,7},{5,4},{7,6},{8,9},{10,11},{9,8... | collective-permute-start | bytes 786440 | tf_op jit(solution)/shard_map/ppermute | solution.py:581
  27.1 7.3 %collective-permute-start.8 = (f32[2,2,128,128]{3,2,1,0:T(8,128)S(1)}, f32[2,2,128,128]{3,2,1,0:T(8,128)S(1)}, u32[]{:S(2)}, u32[]{:S(2)}) collective-permute-start(f32[2,2,128,128]{3,2,1,0:T(8,128)S(1)} %get-tuple-element.47.mine_a), channel_id=1, source_target_pairs={{1,2},{2,1},{5,6},{6,5},{9,10},{10,9},{13,14},{14,13},{17,18},{18,... | collective-permute-start | bytes 786440 | tf_op jit(solution)/shard_map/ppermute | solution.py:581
  27.8 15.2 %collective-permute-start.6 = (f32[2,2,128,128]{3,2,1,0:T(8,128)S(1)}, f32[2,2,128,128]{3,2,1,0:T(8,128)S(1)}, u32[]{:S(2)}, u32[]{:S(2)}) collective-permute-start(f32[2,2,128,128]{3,2,1,0:T(8,128)S(1)} %get-tuple-element.43), channel_id=1, source_target_pairs={{4,8},{12,16},{20,24},{8,4},{16,12},{24,20},{5,9},{13,17},{21,25},... | collective-permute-start | bytes 786440 | tf_op jit(solution)/shard_map/ppermute | solution.py:581
  29.7 13.3 %collective-permute-start.9 = (f32[2,256,128]{2,1,0:T(8,128)S(1)}, f32[2,256,128]{2,1,0:T(8,128)S(1)}, u32[]{:S(2)}, u32[]{:S(2)}) collective-permute-start(f32[2,256,128]{2,1,0:T(8,128)S(1)} %get-tuple-element.48), channel_id=1, source_target_pairs={{1,2},{2,1},{5,6},{6,5},{9,10},{10,9},{13,14},{14,13},{17,18},{18,... | collective-permute-start | bytes 786440 | tf_op jit(solution)/shard_map/ppermute | solution.py:581
  30.4 12.7 %collective-permute-start.10 = (f32[2,256,128]{2,1,0:T(8,128)S(1)}, f32[2,256,128]{2,1,0:T(8,128)S(1)}, u32[]{:S(2)}, u32[]{:S(2)}) collective-permute-start(f32[2,256,128]{2,1,0:T(8,128)S(1)} %get-tuple-element.49), channel_id=1, source_target_pairs={{0,1},{2,3},{1,0},{3,2},{4,5},{6,7},{5,4},{7,6},{8,9},{10,11},{9,8... | collective-permute-start | bytes 786440 | tf_op jit(solution)/shard_map/ppermute | solution.py:581
  34.4 12.6 %collective-permute-start.11 = (f32[2,2,128,128]{3,2,1,0:T(8,128)S(1)}, f32[2,2,128,128]{3,2,1,0:T(8,128)S(1)}, u32[]{:S(2)}, u32[]{:S(2)}) collective-permute-start(f32[2,2,128,128]{3,2,1,0:T(8,128)S(1)} %get-tuple-element.52), channel_id=1, source_target_pairs={{0,4},{8,12},{16,20},{24,28},{4,0},{12,8},{20,16},{28,24},{1,5},{9... | collective-permute-start | bytes 786440 | tf_op jit(solution)/shard_map/ppermute | solution.py:581
  34.5 12.5 %collective-permute-start.12 = (f32[2,2,128,128]{3,2,1,0:T(8,128)S(1)}, f32[2,2,128,128]{3,2,1,0:T(8,128)S(1)}, u32[]{:S(2)}, u32[]{:S(2)}) collective-permute-start(f32[2,2,128,128]{3,2,1,0:T(8,128)S(1)} %shard_map.71), channel_id=1, source_target_pairs={{4,8},{12,16},{20,24},{8,4},{16,12},{24,20},{5,9},{13,17},{21,25},... | collective-permute-start | bytes 786440 | tf_op jit(solution)/shard_map/ppermute | solution.py:581
  43.0 4.1 %collective-permute-start.13 = (f32[2,2,128,128]{3,2,1,0:T(8,128)S(1)}, f32[2,2,128,128]{3,2,1,0:T(8,128)S(1)}, u32[]{:S(2)}, u32[]{:S(2)}) collective-permute-start(f32[2,2,128,128]{3,2,1,0:T(8,128)S(1)} %shard_map.72), channel_id=1, source_target_pairs={{0,4},{8,12},{16,20},{24,28},{4,0},{12,8},{20,16},{28,24},{1,5},{9... | collective-permute-start | bytes 786440 | tf_op jit(solution)/shard_map/ppermute | solution.py:581
  51.7 5.5 %collective-permute-start.14 = (f32[512,128]{1,0:T(8,128)S(1)}, f32[512,128]{1,0:T(8,128)S(1)}, u32[]{:S(2)}, u32[]{:S(2)}) collective-permute-start(f32[512,128]{1,0:T(8,128)S(1)} %get-tuple-element.55), channel_id=1, source_target_pairs={{1,2},{2,1},{5,6},{6,5},{9,10},{10,9},{13,14},{14,13},{17,18},{18,... | collective-permute-start | bytes 786440 | tf_op jit(solution)/shard_map/ppermute | solution.py:581
  52.4 8.8 %collective-permute-start.15 = (f32[512,128]{1,0:T(8,128)S(1)}, f32[512,128]{1,0:T(8,128)S(1)}, u32[]{:S(2)}, u32[]{:S(2)}) collective-permute-start(f32[512,128]{1,0:T(8,128)S(1)} %get-tuple-element.56), channel_id=1, source_target_pairs={{0,1},{2,3},{1,0},{3,2},{4,5},{6,7},{5,4},{7,6},{8,9},{10,11},{9,8... | collective-permute-start | bytes 786440 | tf_op jit(solution)/shard_map/ppermute | solution.py:581
  55.2 10.3 %collective-permute-start.16 = (f32[2,3,64,128]{3,2,1,0:T(8,128)S(1)}, f32[2,3,64,128]{3,2,1,0:T(8,128)S(1)}, u32[]{:S(2)}, u32[]{:S(2)}) collective-permute-start(f32[2,3,64,128]{3,2,1,0:T(8,128)S(1)} %get-tuple-element.57), channel_id=1, source_target_pairs={{4,8},{12,16},{20,24},{8,4},{16,12},{24,20},{5,9},{13,17},{21,25},... | collective-permute-start | bytes 589832 | tf_op jit(solution)/shard_map/ppermute | solution.py:581
  57.1 8.4 %collective-permute-start.17 = (f32[2,3,64,128]{3,2,1,0:T(8,128)S(1)}, f32[2,3,64,128]{3,2,1,0:T(8,128)S(1)}, u32[]{:S(2)}, u32[]{:S(2)}) collective-permute-start(f32[2,3,64,128]{3,2,1,0:T(8,128)S(1)} %get-tuple-element.58), channel_id=1, source_target_pairs={{0,4},{8,12},{16,20},{24,28},{4,0},{12,8},{20,16},{28,24},{1,5},{9... | collective-permute-start | bytes 589832 | tf_op jit(solution)/shard_map/ppermute | solution.py:581
  61.2 5.6 %collective-permute-start.18 = (f32[2,64,128]{2,1,0:T(8,128)S(1)}, f32[2,64,128]{2,1,0:T(8,128)S(1)}, u32[]{:S(2)}, u32[]{:S(2)}) collective-permute-start(f32[2,64,128]{2,1,0:T(8,128)S(1)} %get-tuple-element.59), channel_id=1, source_target_pairs={{4,8},{12,16},{20,24},{8,4},{16,12},{24,20},{5,9},{13,17},{21,25},... | collective-permute-start | bytes 196616 | tf_op jit(solution)/shard_map/ppermute | solution.py:581
  63.2 3.7 %collective-permute-start.19 = (f32[2,64,128]{2,1,0:T(8,128)S(1)}, f32[2,64,128]{2,1,0:T(8,128)S(1)}, u32[]{:S(2)}, u32[]{:S(2)}) collective-permute-start(f32[2,64,128]{2,1,0:T(8,128)S(1)} %get-tuple-element.60), channel_id=1, source_target_pairs={{0,4},{8,12},{16,20},{24,28},{4,0},{12,8},{20,16},{28,24},{1,5},{9... | collective-permute-start | bytes 196616 | tf_op jit(solution)/shard_map/ppermute | solution.py:581

commit v2 on v1

--- a/solution.py
+++ b/solution.py
@@ -125,7 +125,7 @@
     found, _ = collect(chosen, 0, *place, touching)
     found, known = collect(chosen, found, *place, early, GROUP)
     begin = GROUP - jnp.minimum(known, GROUP)
-    end = begin + lax.rem(CHAIN - lax.rem(found, CHAIN), CHAIN)
+    end = begin + lax.rem(GROUP - lax.rem(found, GROUP), GROUP)
     found, _ = collect(chosen, found, *place, clear, begin, end)
     return found, end
 

time: 68.8 us -> 68.4 us (level)
  starting transfers between devices: 33.7 us -> 46.5 us
  Pallas kernels: 28 us -> 18.3 us
  waiting for transfers between devices: 5.35 us -> 2.47 us
    ppermute x20, starting transfers between devices: 33.7 us -> 46.5 us  [swap_pairs(): got.append(lax.ppermute(value, axis, pairs + [(b, a) for a, b in pairs]))]
    pallas_call x1, Pallas kernels: 6.29 us -> 2.7 us  [shards(): call(first_pass, [full, full, tip, tip, strip, strip, edge, edge], 'ss' +...]
    ppermute x20, waiting for transfers between devices: 5.35 us -> 2.47 us  [swap_pairs(): got.append(lax.ppermute(value, axis, pairs + [(b, a) for a, b in pairs]))]
    pallas_call x1, Pallas kernels: 3.96 us -> 1.81 us  [shards(): call(update_pass, [full, full], 'ssa' + 10 * 'v', [chosen], cost(npos // 2))]
    pallas_call x1, Pallas kernels: 4.62 us -> 2.71 us  [shards(): call(second_pass, [full, full, strip, strip, edge, edge], 'ss' + 10 * 'v'...]
    pallas_call x1, Pallas kernels: 4.15 us -> 2.47 us  [shards(): call(functools.partial(light_pass, npos=npos), [(blocks, rows, length)],...]
  transfers between devices with their start and end apart: 20 -> 20, of which waited for: 2 -> 2; matrix products, arithmetic and copies ran while one was open for 0% -> 0% of each run, Pallas kernels for 21% -> 15%
where the time goes in v2:
time: 68.4 us
  starting transfers between devices  46.5 us (68%)
  Pallas kernels  18.3 us (27%)
  waiting for transfers between devices  2.47 us (4%)
  between operations  1.16 us (2%)
    ppermute x20, starting transfers between devices, swap_pairs(): got.append(lax.ppermute(value, axis, pairs + [(b, a) for a, b in pairs]))  46.5 us
    pallas_call x1, Pallas kernels, shards(): call(second_pass, [full, full, strip, strip, edge, edge], 'ss' + 10 * 'v'...  2.71 us
    pallas_call x1, Pallas kernels, shards(): call(first_pass, [full, full, tip, tip, strip, strip, edge, edge], 'ss' +...  2.7 us
    ppermute x20, waiting for transfers between devices, swap_pairs(): got.append(lax.ppermute(value, axis, pairs + [(b, a) for a, b in pairs]))  2.47 us
    pallas_call x1, Pallas kernels, shards(): call(functools.partial(light_pass, npos=npos), [(blocks, rows, length)],...  2.47 us
    pallas_call x1, Pallas kernels, shards(): call(early_pass, [(2, nb, tile, length)], 'ssavvvv', [chosen], cost(GROUP))  2.16 us
    pallas_call x1, Pallas kernels, shards(): call(inner_pass, [own], 'ss' + 4 * 'v', [chosen], cost(npos // 4))  2.11 us
    pallas_call x1, Pallas kernels, shards(): call(update_pass, [full, full], 'ssa' + 10 * 'v', [chosen], cost(npos // 2))  1.81 us
  transfers between devices with their start and end apart: 20, of which 2 were waited for; matrix products, arithmetic and copies ran while one was open for 0% of the time, Pallas kernels for 15%

profile of v2, /device:TPU:1, one launch (start us, length us, event | category | flops | bytes accessed | tf_op | source)
XLA Modules:
  0.0 68.4 jit_solution(4251490765380659361)
XLA Ops:
  0.7 1.5 %shard_map.64 = (f32[2,3,384,128]{3,2,1,0:T(8,128)S(1)}, f32[392,128]{1,0:T(8,128)S(1)}, f32[392,128]{1,0:T(8,128)S(1)}, f32[392,128]{1,0:T(8,128)S(1)}, f32[392,128]{1,0:T(8,128)S(1)}) custom-call(f32[2,384,384]{2,1,0:T(8,128)} %field.1, s32[1,1,2,12]{3,2,1,0:T(2,128)} %bitcast.1, s32[1,1]{1,0:T(1,128)S(6)} %copy.7.counts), custom_call_target="tpu_custom_call" | custom-call | tf_op jit(solution)/shard_map/pallas_call | solution.py:609
  2.2 2.2 %collective-permute-start.1 = (f32[392,128]{1,0:T(8,128)S(1)}, f32[392,128]{1,0:T(8,128)S(1)}, u32[]{:S(2)}, u32[]{:S(2)}) collective-permute-start(f32[392,128]{1,0:T(8,128)S(1)} %get-tuple-element.35), channel_id=1, source_target_pairs={{0,1},{2,3},{1,0},{3,2},{4,5},{6,7},{5,4},{7,6},{8,9},{10,11},{9,8... | collective-permute-start | bytes 602120 | tf_op jit(solution)/shard_map/ppermute | solution.py:581
  4.4 0.7 collective-permute-start
  5.0 4.0 %collective-permute-start.2 = (f32[392,128]{1,0:T(8,128)S(1)}, f32[392,128]{1,0:T(8,128)S(1)}, u32[]{:S(2)}, u32[]{:S(2)}) collective-permute-start(f32[392,128]{1,0:T(8,128)S(1)} %get-tuple-element.40), channel_id=1, source_target_pairs={{4,8},{12,16},{20,24},{8,4},{16,12},{24,20},{5,9},{13,17},{21,25},... | collective-permute-start | bytes 602120 | tf_op jit(solution)/shard_map/ppermute | solution.py:581
  9.0 0.1 collective-permute-start.3
  9.1 1.3 %shard_map.65 = (f32[2,128,128]{2,1,0:T(8,128)S(1)}, f32[1,1,12,128,128]{4,3,2,1,0:T(8,128)S(1)}, bf16[4,256,256]{2,1,0:T(8,128)(2,1)S(1)}) custom-call(f32[392,128]{1,0:T(8,128)S(1)} %get-tuple-element.34.after.mine, f32[2,128,128]{2,1,0:T(8,128)} %probe_from.1, f32[1,1,12,128,128]{4,3,2,1,0:T(8,128)} %amps_from.1, ...), custom_call_target="tpu_custom_call" | custom-call | flops 201326592 | bytes 8000000 | tf_op jit(solution)/shard_map/pallas_call | solution.py:614
  10.4 0.1 shard_map.66
  10.5 3.5 %collective-permute-start.4 = (f32[136,128]{1,0:T(8,128)S(1)}, f32[136,128]{1,0:T(8,128)S(1)}, u32[]{:S(2)}, u32[]{:S(2)}) collective-permute-start(f32[136,128]{1,0:T(8,128)S(1)} %get-tuple-element.42), channel_id=1, source_target_pairs={{4,8},{12,16},{20,24},{8,4},{16,12},{24,20},{5,9},{13,17},{21,25},... | collective-permute-start | bytes 208904 | tf_op jit(solution)/shard_map/ppermute | solution.py:581
  14.1 0.1 collective-permute-start.5
  14.1 2.2 %shard_map.67.done = f32[2,3,384,128]{3,2,1,0:T(8,128)S(1)} custom-call(s32[1,1,2,12]{3,2,1,0:T(2,128)S(1)} %bitcast.2, s32[1,1]{1,0:T(1,128)S(6)} %copy.7.counts, f32[136,128]{1,0:T(8,128)S(1)} %get-tuple-element.37.after, f32[2,3,384,128]{3,2,1,0:T(8,128)S(1)} %get-tuple-element.33.field, f32[2,128,128]{2,1,0:T(8,128)S(1)} %get-tuple-element.36.after.probe, ...), custom_call_target="tpu_custom_call" | custom-call | flops 805306368 | bytes 8000000 | tf_op jit(solution)/shard_map/pallas_call | solution.py:628
  16.4 2.7 %shard_map.68 = (f32[2,5,512,128]{3,2,1,0:T(8,128)S(1)}, f32[2,5,512,128]{3,2,1,0:T(8,128)S(1)}, f32[2,2,128,128]{3,2,1,0:T(8,128)S(1)}, f32[2,2,128,128]{3,2,1,...) custom-call(s32[1,1,2,12]{3,2,1,0:T(2,128)S(1)} %bitcast.3, ...), custom_call_target="tpu_custom_call" | custom-call | tf_op jit(solution)/shard_map/pallas_call | solution.py:638
  19.1 6.8 %collective-permute-start.7 = (f32[2,2,128,128]{3,2,1,0:T(8,128)S(1)}, f32[2,2,128,128]{3,2,1,0:T(8,128)S(1)}, u32[]{:S(2)}, u32[]{:S(2)}) collective-permute-start(f32[2,2,128,128]{3,2,1,0:T(8,128)S(1)} %get-tuple-element.46.mine_b), channel_id=1, source_target_pairs={{0,1},{2,3},{1,0},{3,2},{4,5},{6,7},{5,4},{7,6},{8,9},{10,11},{9,8... | collective-permute-start | bytes 786440 | tf_op jit(solution)/shard_map/ppermute | solution.py:581
  25.8 0.7 collective-permute-start.8
  26.5 1.9 %collective-permute-start.6 = (f32[2,2,128,128]{3,2,1,0:T(8,128)S(1)}, f32[2,2,128,128]{3,2,1,0:T(8,128)S(1)}, u32[]{:S(2)}, u32[]{:S(2)}) collective-permute-start(f32[2,2,128,128]{3,2,1,0:T(8,128)S(1)} %get-tuple-element.43), channel_id=1, source_target_pairs={{4,8},{12,16},{20,24},{8,4},{16,12},{24,20},{5,9},{13,17},{21,25},... | collective-permute-start | bytes 786440 | tf_op jit(solution)/shard_map/ppermute | solution.py:581
  28.4 0.7 collective-permute-start.9
  29.1 5.6 %collective-permute-start.10 = (f32[2,256,128]{2,1,0:T(8,128)S(1)}, f32[2,256,128]{2,1,0:T(8,128)S(1)}, u32[]{:S(2)}, u32[]{:S(2)}) collective-permute-start(f32[2,256,128]{2,1,0:T(8,128)S(1)} %get-tuple-element.49), channel_id=1, source_target_pairs={{0,1},{2,3},{1,0},{3,2},{4,5},{6,7},{5,4},{7,6},{8,9},{10,11},{9,8... | collective-permute-start | bytes 786440 | tf_op jit(solution)/shard_map/ppermute | solution.py:581
  34.7 0.1 shard_map.71
  34.8 4.0 %collective-permute-start.12 = (f32[2,2,128,128]{3,2,1,0:T(8,128)S(1)}, f32[2,2,128,128]{3,2,1,0:T(8,128)S(1)}, u32[]{:S(2)}, u32[]{:S(2)}) collective-permute-start(f32[2,2,128,128]{3,2,1,0:T(8,128)S(1)} %shard_map.71), channel_id=1, source_target_pairs={{4,8},{12,16},{20,24},{8,4},{16,12},{24,20},{5,9},{13,17},{21,25},... | collective-permute-start | bytes 786440 | tf_op jit(solution)/shard_map/ppermute | solution.py:581
  38.9 2.5 %shard_map.69.inverse.after = f32[5,512,128]{2,1,0:T(8,128)S(1)} custom-call(f32[392,128]{1,0:T(8,128)S(1)} %get-tuple-element.34.after.mine, f32[392,128]{1,0:T(8,128)S(1)} %collective-permute-done.cols_a, f32[392,128]{1,0:T(8,128)S(1)} %collective-permute-done.1.cols_b, f32[392,128]{1,0:T(8,128)S(1)} %collective-permute-done.2.rows_a, ...), custom_call_target="tpu_custom_call" | custom-call | flops 1207959552 | bytes 8000000 | tf_op jit(solution)/shard_map/pallas_call | solution.py:647
  41.4 0.1 shard_map.72
  41.5 1.8 %shard_map.70 = (f32[2,5,512,128]{3,2,1,0:T(8,128)S(1)}, f32[2,5,512,128]{3,2,1,0:T(8,128)S(1)}) custom-call(s32[1,1,2,12]{3,2,1,0:T(2,128)S(1)} %bitcast.4, s32[1,1]{1,0:T(1,128)S(6)} %copy.7.counts, f32[2,2,128,128]{3,2,1,0:T(8,128)S(1)} %collective-permute-done.6.after.edges_a, f32[2,5,512,128]{3,2,1,0:T(8,128)S(1)} %get-tuple-element.44.frame, ...), custom_call_target="tpu_custom_call" | custom-call | flops 1207959552 | bytes 8000000 | tf_op jit(solution)/shard_map/pallas_call | solution.py:662
  43.4 1.4 %collective-permute-done.12.corners_a = f32[2,2,128,128]{3,2,1,0:T(8,128)S(1)} collective-permute-done((f32[2,2,128,128]{3,2,1,0:T(8,128)S(1)}, f32[2,2,128,128]{3,2,1,0:T(8,128)S(1)}, u32[]{:S(2)}, u32[]{:S(2)}) %collective-permute-start.12) | collective-permute-done | bytes 262176 | tf_op jit(solution)/shard_map/ppermute | solution.py:581
  44.7 2.7 %shard_map.73 = (f32[2,5,512,128]{3,2,1,0:T(8,128)S(1)}, f32[2,5,512,128]{3,2,1,0:T(8,128)S(1)}, f32[512,128]{1,0:T(8,128)S(1)}, f32[512,128]{1,0:T(8,128)S(1)},...) custom-call(s32[1,1,2,12]{3,2,1,0:T(2,128)S(1)} %bitcast.5, s32[1,1]{1,0:T(1,128)S(6)} %copy.7.counts, ...), custom_call_target="tpu_custom_call" | custom-call | flops 1207959552 | bytes 8000000 | tf_op jit(solution)/shard_map/pallas_call | solution.py:668
  47.5 0.7 collective-permute-start.14
  48.1 5.5 %collective-permute-start.15 = (f32[512,128]{1,0:T(8,128)S(1)}, f32[512,128]{1,0:T(8,128)S(1)}, u32[]{:S(2)}, u32[]{:S(2)}) collective-permute-start(f32[512,128]{1,0:T(8,128)S(1)} %get-tuple-element.56), channel_id=1, source_target_pairs={{0,1},{2,3},{1,0},{3,2},{4,5},{6,7},{5,4},{7,6},{8,9},{10,11},{9,8... | collective-permute-start | bytes 786440 | tf_op jit(solution)/shard_map/ppermute | solution.py:581
  53.6 4.9 %collective-permute-start.16 = (f32[2,3,64,128]{3,2,1,0:T(8,128)S(1)}, f32[2,3,64,128]{3,2,1,0:T(8,128)S(1)}, u32[]{:S(2)}, u32[]{:S(2)}) collective-permute-start(f32[2,3,64,128]{3,2,1,0:T(8,128)S(1)} %get-tuple-element.57), channel_id=1, source_target_pairs={{4,8},{12,16},{20,24},{8,4},{16,12},{24,20},{5,9},{13,17},{21,25},... | collective-permute-start | bytes 589832 | tf_op jit(solution)/shard_map/ppermute | solution.py:581
  58.5 0.1 collective-permute-start.17
  58.6 1.1 %collective-permute-done.15.cols_b = f32[512,128]{1,0:T(8,128)S(1)} collective-permute-done((f32[512,128]{1,0:T(8,128)S(1)}, f32[512,128]{1,0:T(8,128)S(1)}, u32[]{:S(2)}, u32[]{:S(2)}) %collective-permute-start.15) | collective-permute-done | bytes 262176 | tf_op jit(solution)/shard_map/ppermute | solution.py:581
  59.7 5.1 %collective-permute-start.18 = (f32[2,64,128]{2,1,0:T(8,128)S(1)}, f32[2,64,128]{2,1,0:T(8,128)S(1)}, u32[]{:S(2)}, u32[]{:S(2)}) collective-permute-start(f32[2,64,128]{2,1,0:T(8,128)S(1)} %get-tuple-element.59), channel_id=1, source_target_pairs={{4,8},{12,16},{20,24},{8,4},{16,12},{24,20},{5,9},{13,17},{21,25},... | collective-permute-start | bytes 196616 | tf_op jit(solution)/shard_map/ppermute | solution.py:581
  64.8 0.1 collective-permute-start.19
  64.9 2.1 %shard_map.74.inner = f32[2,3,384,128]{3,2,1,0:T(8,128)S(1)} custom-call(s32[1,1,2,12]{3,2,1,0:T(2,128)S(1)} %bitcast.6, s32[1,1]{1,0:T(1,128)S(6)} %copy.7.counts, f32[2,5,512,128]{3,2,1,0:T(8,128)S(1)} %get-tuple-element.53.work, f32[2,128,128]{2,1,0:T(8,128)S(1)} %get-tuple-element.36.after.probe, f32[1,1,12,128,128]{4,3,2,1,0:T(8,128)S(1)} %get-tuple-element.38.amps, ...), custom_call_target="tpu_custom_call" | custom-call | flops 603979776 | bytes 8000000 | tf_op jit(solution)/shard_map/pallas_call | solution.py:675
  67.0 1.2 %shard_map.76 = f32[2,384,384]{2,1,0:T(8,128)} custom-call(f32[2,5,512,128]{3,2,1,0:T(8,128)S(1)} %get-tuple-element.53.work, f32[2,5,512,128]{3,2,1,0:T(8,128)S(1)} %get-tuple-element.54.total, f32[2,3,384,128]{3,2,1,0:T(8,128)S(1)} %shard_map.74.inner, f32[5,512,128]{2,1,0:T(8,128)S(1)} %shard_map.69.inverse.after, ...), custom_call_target="tpu_custom_call" | custom-call | tf_op jit(solution)/shard_map/pallas_call | solution.py:680
  (23 shorter events, 0.1 us)
Async XLA Ops:
  0.0 14.1 %copy-start = (s32[1,1,12,2]{2,3,1,0:T(2,128)S(1)}, s32[1,1,12,2]{2,3,1,0:T(2,128)}, u32[]{:S(2)}) copy-start(s32[1,1,12,2]{2,3,1,0:T(2,128)} %param.9) | copy-start | bytes 292
  2.2 8.2 %collective-permute-start.1 = (f32[392,128]{1,0:T(8,128)S(1)}, f32[392,128]{1,0:T(8,128)S(1)}, u32[]{:S(2)}, u32[]{:S(2)}) collective-permute-start(f32[392,128]{1,0:T(8,128)S(1)} %get-tuple-element.35), channel_id=1, source_target_pairs={{0,1},{2,3},{1,0},{3,2},{4,5},{6,7},{5,4},{7,6},{8,9},{10,11},{9,8... | collective-permute-start | bytes 602120 | tf_op jit(solution)/shard_map/ppermute | solution.py:581
  4.4 6.1 %collective-permute-start = (f32[392,128]{1,0:T(8,128)S(1)}, f32[392,128]{1,0:T(8,128)S(1)}, u32[]{:S(2)}, u32[]{:S(2)}) collective-permute-start(f32[392,128]{1,0:T(8,128)S(1)} %get-tuple-element.34.after.mine), channel_id=1, source_target_pairs={{1,2},{2,1},{5,6},{6,5},{9,10},{10,9},{13,14},{14,13},{17,18},{18,... | collective-permute-start | bytes 602120 | tf_op jit(solution)/shard_map/ppermute | solution.py:581
  5.0 11.3 %collective-permute-start.2 = (f32[392,128]{1,0:T(8,128)S(1)}, f32[392,128]{1,0:T(8,128)S(1)}, u32[]{:S(2)}, u32[]{:S(2)}) collective-permute-start(f32[392,128]{1,0:T(8,128)S(1)} %get-tuple-element.40), channel_id=1, source_target_pairs={{4,8},{12,16},{20,24},{8,4},{16,12},{24,20},{5,9},{13,17},{21,25},... | collective-permute-start | bytes 602120 | tf_op jit(solution)/shard_map/ppermute | solution.py:581
  9.0 7.3 %collective-permute-start.3 = (f32[392,128]{1,0:T(8,128)S(1)}, f32[392,128]{1,0:T(8,128)S(1)}, u32[]{:S(2)}, u32[]{:S(2)}) collective-permute-start(f32[392,128]{1,0:T(8,128)S(1)} %get-tuple-element.41), channel_id=1, source_target_pairs={{0,4},{8,12},{16,20},{24,28},{4,0},{12,8},{20,16},{28,24},{1,5},{9... | collective-permute-start | bytes 602120 | tf_op jit(solution)/shard_map/ppermute | solution.py:581
  10.5 5.8 %collective-permute-start.4 = (f32[136,128]{1,0:T(8,128)S(1)}, f32[136,128]{1,0:T(8,128)S(1)}, u32[]{:S(2)}, u32[]{:S(2)}) collective-permute-start(f32[136,128]{1,0:T(8,128)S(1)} %get-tuple-element.42), channel_id=1, source_target_pairs={{4,8},{12,16},{20,24},{8,4},{16,12},{24,20},{5,9},{13,17},{21,25},... | collective-permute-start | bytes 208904 | tf_op jit(solution)/shard_map/ppermute | solution.py:581
  14.1 2.3 %collective-permute-start.5 = (f32[136,128]{1,0:T(8,128)S(1)}, f32[136,128]{1,0:T(8,128)S(1)}, u32[]{:S(2)}, u32[]{:S(2)}) collective-permute-start(f32[136,128]{1,0:T(8,128)S(1)} %get-tuple-element.37.after), channel_id=1, source_target_pairs={{0,4},{8,12},{16,20},{24,28},{4,0},{12,8},{20,16},{28,24},{1,5},{9... | collective-permute-start | bytes 208904 | tf_op jit(solution)/shard_map/ppermute | solution.py:581
  19.1 15.7 %collective-permute-start.7 = (f32[2,2,128,128]{3,2,1,0:T(8,128)S(1)}, f32[2,2,128,128]{3,2,1,0:T(8,128)S(1)}, u32[]{:S(2)}, u32[]{:S(2)}) collective-permute-start(f32[2,2,128,128]{3,2,1,0:T(8,128)S(1)} %get-tuple-element.46.mine_b), channel_id=1, source_target_pairs={{0,1},{2,3},{1,0},{3,2},{4,5},{6,7},{5,4},{7,6},{8,9},{10,11},{9,8... | collective-permute-start | bytes 786440 | tf_op jit(solution)/shard_map/ppermute | solution.py:581
  25.8 8.9 %collective-permute-start.8 = (f32[2,2,128,128]{3,2,1,0:T(8,128)S(1)}, f32[2,2,128,128]{3,2,1,0:T(8,128)S(1)}, u32[]{:S(2)}, u32[]{:S(2)}) collective-permute-start(f32[2,2,128,128]{3,2,1,0:T(8,128)S(1)} %get-tuple-element.47.mine_a), channel_id=1, source_target_pairs={{1,2},{2,1},{5,6},{6,5},{9,10},{10,9},{13,14},{14,13},{17,18},{18,... | collective-permute-start | bytes 786440 | tf_op jit(solution)/shard_map/ppermute | solution.py:581
  26.5 14.9 %collective-permute-start.6 = (f32[2,2,128,128]{3,2,1,0:T(8,128)S(1)}, f32[2,2,128,128]{3,2,1,0:T(8,128)S(1)}, u32[]{:S(2)}, u32[]{:S(2)}) collective-permute-start(f32[2,2,128,128]{3,2,1,0:T(8,128)S(1)} %get-tuple-element.43), channel_id=1, source_target_pairs={{4,8},{12,16},{20,24},{8,4},{16,12},{24,20},{5,9},{13,17},{21,25},... | collective-permute-start | bytes 786440 | tf_op jit(solution)/shard_map/ppermute | solution.py:581
  28.4 13.1 %collective-permute-start.9 = (f32[2,256,128]{2,1,0:T(8,128)S(1)}, f32[2,256,128]{2,1,0:T(8,128)S(1)}, u32[]{:S(2)}, u32[]{:S(2)}) collective-permute-start(f32[2,256,128]{2,1,0:T(8,128)S(1)} %get-tuple-element.48), channel_id=1, source_target_pairs={{1,2},{2,1},{5,6},{6,5},{9,10},{10,9},{13,14},{14,13},{17,18},{18,... | collective-permute-start | bytes 786440 | tf_op jit(solution)/shard_map/ppermute | solution.py:581
  29.1 12.4 %collective-permute-start.10 = (f32[2,256,128]{2,1,0:T(8,128)S(1)}, f32[2,256,128]{2,1,0:T(8,128)S(1)}, u32[]{:S(2)}, u32[]{:S(2)}) collective-permute-start(f32[2,256,128]{2,1,0:T(8,128)S(1)} %get-tuple-element.49), channel_id=1, source_target_pairs={{0,1},{2,3},{1,0},{3,2},{4,5},{6,7},{5,4},{7,6},{8,9},{10,11},{9,8... | collective-permute-start | bytes 786440 | tf_op jit(solution)/shard_map/ppermute | solution.py:581
  34.7 8.6 %collective-permute-start.11 = (f32[2,2,128,128]{3,2,1,0:T(8,128)S(1)}, f32[2,2,128,128]{3,2,1,0:T(8,128)S(1)}, u32[]{:S(2)}, u32[]{:S(2)}) collective-permute-start(f32[2,2,128,128]{3,2,1,0:T(8,128)S(1)} %get-tuple-element.52), channel_id=1, source_target_pairs={{0,4},{8,12},{16,20},{24,28},{4,0},{12,8},{20,16},{28,24},{1,5},{9... | collective-permute-start | bytes 786440 | tf_op jit(solution)/shard_map/ppermute | solution.py:581
  34.8 9.9 %collective-permute-start.12 = (f32[2,2,128,128]{3,2,1,0:T(8,128)S(1)}, f32[2,2,128,128]{3,2,1,0:T(8,128)S(1)}, u32[]{:S(2)}, u32[]{:S(2)}) collective-permute-start(f32[2,2,128,128]{3,2,1,0:T(8,128)S(1)} %shard_map.71), channel_id=1, source_target_pairs={{4,8},{12,16},{20,24},{8,4},{16,12},{24,20},{5,9},{13,17},{21,25},... | collective-permute-start | bytes 786440 | tf_op jit(solution)/shard_map/ppermute | solution.py:581
  41.4 3.3 %collective-permute-start.13 = (f32[2,2,128,128]{3,2,1,0:T(8,128)S(1)}, f32[2,2,128,128]{3,2,1,0:T(8,128)S(1)}, u32[]{:S(2)}, u32[]{:S(2)}) collective-permute-start(f32[2,2,128,128]{3,2,1,0:T(8,128)S(1)} %shard_map.72), channel_id=1, source_target_pairs={{0,4},{8,12},{16,20},{24,28},{4,0},{12,8},{20,16},{28,24},{1,5},{9... | collective-permute-start | bytes 786440 | tf_op jit(solution)/shard_map/ppermute | solution.py:581
  47.5 11.1 %collective-permute-start.14 = (f32[512,128]{1,0:T(8,128)S(1)}, f32[512,128]{1,0:T(8,128)S(1)}, u32[]{:S(2)}, u32[]{:S(2)}) collective-permute-start(f32[512,128]{1,0:T(8,128)S(1)} %get-tuple-element.55), channel_id=1, source_target_pairs={{1,2},{2,1},{5,6},{6,5},{9,10},{10,9},{13,14},{14,13},{17,18},{18,... | collective-permute-start | bytes 786440 | tf_op jit(solution)/shard_map/ppermute | solution.py:581
  48.1 11.5 %collective-permute-start.15 = (f32[512,128]{1,0:T(8,128)S(1)}, f32[512,128]{1,0:T(8,128)S(1)}, u32[]{:S(2)}, u32[]{:S(2)}) collective-permute-start(f32[512,128]{1,0:T(8,128)S(1)} %get-tuple-element.56), channel_id=1, source_target_pairs={{0,1},{2,3},{1,0},{3,2},{4,5},{6,7},{5,4},{7,6},{8,9},{10,11},{9,8... | collective-permute-start | bytes 786440 | tf_op jit(solution)/shard_map/ppermute | solution.py:581
  53.6 13.4 %collective-permute-start.16 = (f32[2,3,64,128]{3,2,1,0:T(8,128)S(1)}, f32[2,3,64,128]{3,2,1,0:T(8,128)S(1)}, u32[]{:S(2)}, u32[]{:S(2)}) collective-permute-start(f32[2,3,64,128]{3,2,1,0:T(8,128)S(1)} %get-tuple-element.57), channel_id=1, source_target_pairs={{4,8},{12,16},{20,24},{8,4},{16,12},{24,20},{5,9},{13,17},{21,25},... | collective-permute-start | bytes 589832 | tf_op jit(solution)/shard_map/ppermute | solution.py:581
  58.5 8.5 %collective-permute-start.17 = (f32[2,3,64,128]{3,2,1,0:T(8,128)S(1)}, f32[2,3,64,128]{3,2,1,0:T(8,128)S(1)}, u32[]{:S(2)}, u32[]{:S(2)}) collective-permute-start(f32[2,3,64,128]{3,2,1,0:T(8,128)S(1)} %get-tuple-element.58), channel_id=1, source_target_pairs={{0,4},{8,12},{16,20},{24,28},{4,0},{12,8},{20,16},{28,24},{1,5},{9... | collective-permute-start | bytes 589832 | tf_op jit(solution)/shard_map/ppermute | solution.py:581
  59.7 7.3 %collective-permute-start.18 = (f32[2,64,128]{2,1,0:T(8,128)S(1)}, f32[2,64,128]{2,1,0:T(8,128)S(1)}, u32[]{:S(2)}, u32[]{:S(2)}) collective-permute-start(f32[2,64,128]{2,1,0:T(8,128)S(1)} %get-tuple-element.59), channel_id=1, source_target_pairs={{4,8},{12,16},{20,24},{8,4},{16,12},{24,20},{5,9},{13,17},{21,25},... | collective-permute-start | bytes 196616 | tf_op jit(solution)/shard_map/ppermute | solution.py:581
  64.8 2.2 %collective-permute-start.19 = (f32[2,64,128]{2,1,0:T(8,128)S(1)}, f32[2,64,128]{2,1,0:T(8,128)S(1)}, u32[]{:S(2)}, u32[]{:S(2)}) collective-permute-start(f32[2,64,128]{2,1,0:T(8,128)S(1)} %get-tuple-element.60), channel_id=1, source_target_pairs={{0,4},{8,12},{16,20},{24,28},{4,0},{12,8},{20,16},{28,24},{1,5},{9... | collective-permute-start | bytes 196616 | tf_op jit(solution)/shard_map/ppermute | solution.py:581
